TPU v7x, 128 devices: a whole 4x4x4 slice. The times are simulated.
128 devices in a mesh: ty: 8 (over y, core), tx: 16 (over x, z).
Axes of the slice: x: 4, y: 4, z: 4, core: 2. Of those that a mesh axis runs over, the one named last changes fastest.
Arguments:
- locations: float32 [8, 16, 3, 65536], P('ty', 'tx'), may hold values from -2.5 to 2.5
- solution: float32 [8, 16, 65536], P('ty', 'tx'), may hold values from -0.5 to 0.5
- cotangent: float32 [8, 16, 65536], P('ty', 'tx'), may hold values from -6 to 6
- block_fill: int32 [8, 16, 256], P('ty', 'tx'), may hold values from 64 to 256
- pair_own: int32 [8, 16, 192], P('ty', 'tx'), may hold values from 0 to 255
- pair_offset: int32 [8, 16, 192], P('ty', 'tx'), may hold values from 0 to 8, as said below
- pair_block: int32 [8, 16, 192], P('ty', 'tx'), may hold values from 0 to 255
- pair_count: int32 [8, 16], P('ty', 'tx'), may hold values from 24 to 192, as said below
Outputs:
- location_gradient: float32 [8, 16, 3, 65536], P('ty', 'tx')
Inputs may be any that keep to these rules, and one draw needn't show every extreme that they name: `pair_offset`: the partner tile always lies inside the grid of 8 x 16 tiles. `pair_count`: slots at and past a tile's count carry no pair. Some tile fills all 192 slots.
All inputs are finite; a program needn't handle non-finite values.
Results may differ from a plain program's by a relative error of at most 0.0003.
Values sent between devices are 32-bit elements; how exact they have to be, the bound alone decides.
No kernel may reach another device: no remote copies, remote signals or barrier semaphores. Data moves between devices by JAX's collectives and lax.ppermute only.
A program may use at most 128 MiB of HBM per device.

v0:
```python
import jax
import jax.numpy as jnp
from jax import lax
from jax.experimental import pallas as pl
from jax.experimental.pallas import tpu as pltpu
from jax.sharding import PartitionSpec as P

lanes = 128
halves = 2
fields = 5
axes = 3
meta_rows = 8
kinds = 5
kept = 32
bf16 = jnp.bfloat16
f32 = jnp.float32
i32 = jnp.int32


def third(heading):
    return (heading * 11) >> 5


def note_kernel(count_ref, fill_ref, own_ref, offset_ref, block_ref, note_ref, count_s, fill_v, lists_v, sem):
    copies = (
        pltpu.make_async_copy(fill_ref, fill_v, sem.at[0]),
        pltpu.make_async_copy(own_ref, lists_v.at[0], sem.at[1]),
        pltpu.make_async_copy(offset_ref, lists_v.at[1], sem.at[2]),
        pltpu.make_async_copy(block_ref, lists_v.at[2], sem.at[3]),
        pltpu.make_async_copy(count_ref, count_s, sem.at[4]),
    )
    for c in copies:
        c.start()
    for c in copies:
        c.wait()
    own, offset, block = (wide(lists_v[k]) for k in range(3))
    last = lax.broadcasted_iota(i32, own.shape, 1) == own.shape[1] - 1
    own = jnp.where(last, count_s[0, 0], own)
    note_ref[...] = jnp.concatenate([two_rows(x) for x in (fill_v[...], own, offset, block)], axis=0).astype(f32)


def lists_of(ref, rows):
    meta = ref[fields * rows : fields * rows + meta_rows, :].astype(i32)
    parts = [one_row(meta[2 * k : 2 * k + 2]) for k in range(4)]
    return (*parts, parts[1][:, halves * lanes - 1 :])


def rows_dot(x, y, contract):
    return lax.dot_general(x.astype(bf16), y.astype(bf16), (((1,), (contract,)), ((), ())), preferred_element_type=f32)


def split3(x):
    high = x.astype(bf16).astype(f32)
    rest = x - high
    mid = rest.astype(bf16).astype(f32)
    return high, mid, rest - mid


def stacked(rows, width):
    rows = [r.astype(f32) for r in rows]
    return jnp.concatenate(rows + [jnp.zeros((8 - len(rows), width), f32)], axis=0)


def wide(row):
    missing = halves * lanes - row.shape[1]
    return row if missing == 0 else jnp.concatenate([row, jnp.zeros((1, missing), row.dtype)], axis=1)


def one_row(x):
    return jnp.concatenate([x[0:1], x[1:2]], axis=1)


def two_rows(x):
    return jnp.concatenate([x[:, h * lanes : (h + 1) * lanes] for h in range(x.shape[1] // lanes)], axis=0)


def equal_rows(row, count, first=0):
    at = lax.broadcasted_iota(i32, (count, row.shape[1]), 0) + first
    return (row.astype(i32) == at).astype(f32).astype(bf16)


def running(flags):
    size = halves * lanes
    upper = lax.broadcasted_iota(i32, (size, size), 0) <= lax.broadcasted_iota(i32, (size, size), 1)
    return rows_dot(flags, upper.astype(f32), 0)


def pack_kernel(slots, rows, tile_ref, east_ref, west_ref, origin_ref):
    blocks = rows // halves
    size = halves * lanes
    slot_rows = halves * slots
    fill, own, offset, block, count = lists_of(tile_ref, rows)
    live = lax.broadcasted_iota(i32, (1, size), 1) < count
    dr = third(offset)
    dc = offset - 3 * dr
    marks = [live & (dc == want) for want in (2, 0)]
    counts = running(stacked(marks, size))
    picked = equal_rows(own, blocks)
    fill = rows_dot(stacked([fill], size), picked, 0)[0:1]
    values = stacked([block, fill, dr, own + 1], size)
    lane_id = lax.broadcasted_iota(i32, (1, lanes), 1)
    chosen = []
    for side, out_ref in enumerate((east_ref, west_ref)):
        count = counts[side : side + 1]
        place = jnp.where(marks[side], count - 1.0, -1.0)
        moved = equal_rows(place, slots)
        meta = rows_dot(values, moved, 1)
        meta = jnp.concatenate([meta, jnp.zeros((8, size - slots), f32)], axis=1)
        ends = jnp.where(lane_id == 0, count[:, size - 1 :], 0.0)
        out_ref[fields * slot_rows : fields * slot_rows + meta_rows, :] = jnp.concatenate(
            [two_rows(meta[k : k + 1]) for k in range(3)] + [ends, jnp.zeros((1, lanes), f32)], axis=0)
        origin_ref[side : side + 1, :] = meta[3:4] - 1.0
        chosen.append(rows_dot(moved, picked, 1).astype(bf16))
    for f in range(fields):
        data = jnp.concatenate([tile_ref[pl.ds(f * rows + h, blocks, stride=halves), :] for h in range(halves)], axis=1)
        parts = split3(data)
        for pick, out_ref in zip(chosen, (east_ref, west_ref)):
            got = rows_dot(pick, parts[0], 0) + rows_dot(pick, parts[1], 0) + rows_dot(pick, parts[2], 0)
            for h in range(halves):
                out_ref[pl.ds(f * slot_rows + h, slots, stride=halves), :] = got[:, h * lanes : (h + 1) * lanes]


def shape_of(kind):
    steps = (16, 24, 16, 24, 32)[kind]
    return steps, -(-steps // 16), (1, 1, 2, 2, 2)[kind]


def pair_loops(total, spare, table, src, grad, buffers):
    size = halves * lanes

    def word_at(k, at):
        place = table[11, k] + at
        return table[12 + (place >> 7), place & 127]

    def load(index, fill, parts):
        size = parts * lanes
        row_id = lax.broadcasted_iota(i32, (8, size), 0)
        lane_id = lax.broadcasted_iota(i32, (8, size), 1)
        pieces = []
        for h in range(parts):
            got = src[pl.ds(halves * index + h, fields, stride=total), :]
            pieces.append(jnp.concatenate([got, jnp.zeros((8 - fields, lanes), f32)], axis=0))
        x = jnp.concatenate(pieces, axis=1)
        return jnp.where((row_id < axes) | (lane_id < fill), x, 0.0)

    def spread(k, at, mixed, partner):
        steps, parts_a, parts_b = shape_of(k)
        word = word_at(k, at)
        ia, ib = word & 4095, word >> 12
        live = at < table[11, 8 + k]
        a = load(ia, jnp.where(live, table[ia >> 7, ia & 127], 0), parts_a)
        b = load(ib, jnp.where(live, table[ib >> 7, ib & 127], 0), parts_b)
        partner[:, : parts_b * lanes] = b
        zero = jnp.zeros((8, lanes), f32)
        row_b = lax.broadcasted_iota(i32, b.shape, 0)
        ah, am, al = split3(a)
        left = jnp.concatenate([ah, am, al, ah], axis=0).astype(bf16)
        swapped = jnp.where(row_b == 3, jnp.roll(b, -1, axis=0), jnp.where(row_b == 4, jnp.roll(b, 1, axis=0), 0.0))
        swapped = swapped * -20.0
        sh = swapped.astype(bf16).astype(f32)
        sm = swapped - sh
        right = jnp.concatenate([sh, sh, jnp.zeros_like(b), sm], axis=0).astype(bf16)
        row_id = lax.broadcasted_iota(i32, (8, lanes), 0)
        units = [(row_id == f).astype(f32) for f in range(axes)]
        pick = jnp.concatenate([jnp.concatenate([u, u, u, zero], axis=0) for u in units], axis=1).astype(bf16)
        mixed[: parts_a * lanes, : (axes + parts_b) * lanes] = lax.dot_general(
            left, jnp.concatenate([pick, right], axis=1), (((0,), (0,)), ((), ())), preferred_element_type=f32)

    def work(k, mixed, partner, own, far):
        steps, parts_a, parts_b = shape_of(k)
        b_rows = [
            [jnp.broadcast_to(partner[f : f + 1, p * lanes : (p + 1) * lanes], (8, lanes)) for f in range(axes)]
            for p in range(parts_b)
        ]
        sums = [[None] * axes for _ in range(parts_b)]
        for g in range(steps):
            rows = slice(8 * g, 8 * g + 8)
            a_cols = [mixed[rows, f * lanes : (f + 1) * lanes] for f in range(axes)]
            mine = [None] * axes
            for p in range(parts_b):
                diff = [a_cols[f] - b_rows[p][f] for f in range(axes)]
                square = diff[0] * diff[0] + diff[1] * diff[1] + diff[2] * diff[2]
                square = jnp.maximum(square, 1e-30)
                reach = jnp.maximum(1.0 - square * lax.rsqrt(square), 0.0)
                w = (reach * reach) * (reach * mixed[rows, (axes + p) * lanes : (axes + p + 1) * lanes])
                for f in range(axes):
                    push = w * diff[f]
                    mine[f] = push if p == 0 else mine[f] + push
                    sums[p][f] = push if g == 0 else sums[p][f] + push
            for f in range(axes):
                own[f * size + 8 * g : f * size + 8 * g + 8, :] = mine[f]
        for p in range(parts_b):
            for f in range(axes):
                far[8 * f : 8 * f + 8, p * lanes : (p + 1) * lanes] = sums[p][f]

    def finish(k, at, own, far):
        steps, parts_a, parts_b = shape_of(k)
        word = jnp.where(at < 0, spare | (spare << 12), word_at(k, jnp.maximum(at, 0)))
        ia, ib = word & 4095, word >> 12
        for h in range(parts_a):
            count = min(lanes, 8 * steps - h * lanes)
            rows = []
            for f in range(axes):
                part = own[f * size + h * lanes : f * size + h * lanes + count, :]
                if count < lanes:
                    part = jnp.concatenate([part, jnp.zeros((lanes - count, lanes), f32)], axis=0)
                rows.append(jnp.sum(part.T, axis=0, keepdims=True))
            place = pl.ds(halves * ia + h, axes, stride=total)
            grad[place, :] = grad[place, :] + jnp.concatenate(rows, axis=0)
        for p in range(parts_b):
            rows = [jnp.sum(far[8 * f : 8 * f + 8, p * lanes : (p + 1) * lanes], axis=0, keepdims=True) for f in range(axes)]
            place = pl.ds(halves * ib + p, axes, stride=total)
            grad[place, :] = grad[place, :] - jnp.concatenate(rows, axis=0)

    mixed0, mixed1, partner0, partner1, own0, own1, far0, far1 = buffers
    for k in range(kinds):
        turns = (table[11, 8 + k] + 1) // 2

        def turn(t, carry, k=k):
            at = 2 * t
            finish(k, at - 1, own1, far1)
            work(k, mixed0, partner0, own0, far0)
            spread(k, at + 1, mixed1, partner1)
            finish(k, at, own0, far0)
            work(k, mixed1, partner1, own1, far1)
            spread(k, at + 2, mixed0, partner0)
            return carry

        @pl.when(turns > 0)
        def _(k=k, turns=turns, turn=turn):
            spread(k, 0, mixed0, partner0)
            lax.fori_loop(0, turns, turn, 0)
            finish(k, 2 * turns - 1, own1, far1)


def sorted_pairs(entries):
    size = halves * lanes
    found = []
    for a, b, fill_a, fill_b, live in entries:
        size_a, size_b = (fill_a + 63) >> 6, (fill_b + 63) >> 6
        two_a, two_b = (size_a > 2).astype(i32), (size_b > 2).astype(i32)
        swap = (size_a * (1 + two_b) > size_b * (1 + two_a)) | ((size_a > 3) & (size_b < 3))
        a, b = jnp.where(swap, b, a), jnp.where(swap, a, b)
        size_a, size_b = jnp.where(swap, size_b, size_a), jnp.where(swap, size_a, size_b)
        kind = jnp.maximum(size_a - 2, 0) + jnp.where(size_b > 2, 2, 0)
        marks = [live & (kind == k) for k in range(kinds)]
        counts = running(stacked(marks, size))
        values = stacked([a & 255, a >> 8, b & 255, b >> 8], size)
        found.append((marks, counts, values))
    firsts, totals = [], []
    at = jnp.zeros((1, 1), f32)
    for k in range(kinds):
        firsts.append(at)
        total = sum(counts[k : k + 1, size - 1 :] for _, counts, _ in found)
        totals.append(total)
        at = at + total
    length = size * len(entries)
    ordered = jnp.zeros((8, length), f32)
    before = firsts
    for marks, counts, values in found:
        place = jnp.full((1, size), -1.0, f32)
        for k in range(kinds):
            place = jnp.where(marks[k], before[k] + counts[k : k + 1] - 1.0, place)
        before = [before[k] + counts[k : k + 1, size - 1 :] for k in range(kinds)]
        ordered = ordered + rows_dot(values, equal_rows(place, length), 1)
    ordered = ordered.astype(i32)
    words = ordered[0:1] + (ordered[1:2] << 8) + (ordered[2:3] << 12) + (ordered[3:4] << 20)
    lane_id = lax.broadcasted_iota(i32, (1, lanes), 1)
    bounds = jnp.zeros((1, lanes), i32)
    firsts, totals = [f.astype(i32) for f in firsts], [t.astype(i32) for t in totals]
    for k in (0, 2, 3):
        odd = totals[k] & 1
        totals[k], firsts[k + 1], totals[k + 1] = totals[k] - odd, firsts[k + 1] - odd, totals[k + 1] + odd
    for k in range(kinds):
        bounds = jnp.where(lane_id == k, firsts[k], bounds)
        bounds = jnp.where(lane_id == 8 + k, totals[k], bounds)
    return words, bounds


def as_table(pieces, table_v, table, sem):
    at = 0
    for piece in pieces:
        table_v[at : at + piece.shape[0], :] = piece
        at += piece.shape[0]
    copy = pltpu.make_async_copy(table_v, table, sem)
    copy.start()
    return copy


def fills_of(fills, block):
    return rows_dot(stacked(fills, block.shape[1]), equal_rows(block, halves * lanes), 0).astype(i32)


def column_shares(lists, row, last_row):
    fill, own, offset, block, count = lists
    size = halves * lanes
    live = lax.broadcasted_iota(i32, (1, size), 1) < count
    dr = third(offset)
    column = live & (offset - 3 * dr == 1)
    marks = [column & (dr == k) for k in range(3)]
    rank = running(stacked(marks, size)).astype(i32)
    odd = [(rank[k : k + 1] & 1) == 1 for k in range(3)]
    spare = marks[1] & (rank[1:2] > kept)
    has_north, has_south = row > 0, row < last_row
    to_north = spare & has_north & odd[1]
    to_south = spare & has_south & jnp.logical_not(odd[1])
    inside = marks[1] & jnp.logical_not(to_north | to_south)
    return (
        (marks[0] & odd[0], inside, marks[2] & odd[2]),
        ((marks[0] & jnp.logical_not(odd[0])), to_north),
        ((marks[2] & jnp.logical_not(odd[2])), to_south),
    )


def column_entries(lists, base_row, fills):
    fill, own, offset, block, count = lists
    size = halves * lanes
    a = base_row * size + own
    target = base_row + third(offset) - 1
    b = target * size + block
    near = fills_of(fills, block)
    fill_b = jnp.where(target == 0, near[0:1], jnp.where(target == 1, near[1:2], near[2:3]))
    return a, b, fills_of([fill], own)[0:1], fill_b


def level_kernel(rows, total, last_row, tile_ref, g_tile, src, grad, table_v, table, sem, *buffers):
    blocks = rows // halves
    lists = lists_of(tile_ref, rows)
    mine, _, _ = column_shares(lists, lax.axis_index("ty"), last_row)
    fills = [jnp.zeros_like(lists[0]), lists[0], jnp.zeros_like(lists[0])]
    words, bounds = sorted_pairs([(*column_entries(lists, 1, fills), mine[1])])
    copy = as_table((*map(two_rows, fills), jnp.zeros((5, lanes), i32), bounds, two_rows(words)), table_v, table, sem)
    for f in range(fields):
        src[f * total + rows : f * total + 2 * rows, :] = tile_ref[f * rows : (f + 1) * rows, :]
    for f in range(axes):
        grad[f * total + rows : f * total + 2 * rows, :] = jnp.zeros((rows, lanes), f32)
    copy.wait()
    pair_loops(total, 3 * blocks, table, src, grad, buffers)
    for f in range(axes):
        g_tile[f * rows : (f + 1) * rows, :] = grad[f * total + rows : f * total + 2 * rows, :]


def column_kernel(rows, total, last_row, tile_ref, north_ref, south_ref, start_ref, g_tile, g_north, g_south,
                  src, grad, table_v, table, sem, *buffers):
    blocks = rows // halves
    row = lax.axis_index("ty")
    lists = [lists_of(ref, rows) for ref in (north_ref, tile_ref, south_ref)]
    fills = [l[0] for l in lists]
    shares = [column_shares(l, row + k - 1, last_row) for k, l in enumerate(lists)]
    wanted = (
        shares[0][2][0] | shares[0][2][1],
        shares[1][0][0] | shares[1][0][2],
        shares[2][1][0] | shares[2][1][1],
    )
    words, bounds = sorted_pairs([(*column_entries(l, k, fills), wanted[k]) for k, l in enumerate(lists)])
    copy = as_table((*map(two_rows, fills), jnp.zeros((5, lanes), i32), bounds, two_rows(words)), table_v, table, sem)
    for ref, base in ((north_ref, 0), (tile_ref, rows), (south_ref, 2 * rows)):
        for f in range(fields):
            src[f * total + base : f * total + base + rows, :] = ref[f * rows : (f + 1) * rows, :]
    for f in range(axes):
        grad[f * total : f * total + rows, :] = jnp.zeros((rows, lanes), f32)
        grad[f * total + rows : f * total + 2 * rows, :] = start_ref[f * rows : (f + 1) * rows, :]
        grad[f * total + 2 * rows : f * total + 3 * rows, :] = jnp.zeros((rows, lanes), f32)
    copy.wait()
    pair_loops(total, 3 * blocks, table, src, grad, buffers)
    for ref, base in ((g_north, 0), (g_tile, rows), (g_south, 2 * rows)):
        for f in range(axes):
            ref[f * rows : (f + 1) * rows, :] = grad[f * total + base : f * total + base + rows, :]


def side_kernel(slots, rows, total, tiles, east_ref, west_ref, g_tiles, o_tiles, o_east, o_west,
                src, grad, table_v, table, sem, *buffers):
    blocks = rows // halves
    slot_rows = halves * slots
    size = halves * lanes
    bases = (0, rows, 2 * rows)
    fills = [lists_of(t, rows)[0] for t in tiles]
    east_base, west_base = 6 * lanes, 8 * lanes
    slot_id = lax.broadcasted_iota(i32, (1, size), 1)
    entries, slot_fills = [], []
    for ref, base in ((east_ref, east_base), (west_ref, west_base)):
        meta = ref[fields * slot_rows : fields * slot_rows + meta_rows, :].astype(i32)
        live = slot_id < meta[6:7, 0:1]
        block, fill, dr = (jnp.where(live, one_row(meta[2 * k : 2 * k + 2]), 0) for k in range(3))
        near = fills_of(fills, block)
        fill_b = jnp.where(dr == 0, near[0:1], jnp.where(dr == 1, near[1:2], near[2:3]))
        entries.append((base + slot_id, dr * blocks + block, fill, fill_b, live))
        slot_fills.append(fill)
    words, bounds = sorted_pairs(entries)
    copy = as_table((*map(two_rows, fills), *map(two_rows, slot_fills), jnp.zeros((1, lanes), i32), bounds, two_rows(words)),
                    table_v, table, sem)
    slot_places = ((east_ref, halves * east_base), (west_ref, halves * west_base))
    for ref, base in zip(tiles, bases):
        for f in range(fields):
            src[f * total + base : f * total + base + rows, :] = ref[f * rows : (f + 1) * rows, :]
    for ref, base in slot_places:
        for f in range(fields):
            src[f * total + base : f * total + base + slot_rows, :] = ref[f * slot_rows : (f + 1) * slot_rows, :]
    for ref, base in zip(g_tiles, bases):
        for f in range(axes):
            grad[f * total + base : f * total + base + rows, :] = ref[f * rows : (f + 1) * rows, :]
    for _, base in slot_places:
        for f in range(axes):
            grad[f * total + base : f * total + base + slot_rows, :] = jnp.zeros((slot_rows, lanes), f32)
    copy.wait()
    pair_loops(total, 10 * lanes, table, src, grad, buffers)
    for ref, base in zip(o_tiles, bases):
        for f in range(axes):
            ref[f * rows : (f + 1) * rows, :] = grad[f * total + base : f * total + base + rows, :]
    for ref, (_, base) in zip((o_east, o_west), slot_places):
        for f in range(axes):
            ref[f * slot_rows : (f + 1) * slot_rows, :] = grad[f * total + base : f * total + base + slot_rows, :]


def merge_kernel(slots, rows, origin_ref, g_tile, g_north, g_south, g_east, g_west, out_ref):
    blocks = rows // halves
    slot_rows = halves * slots
    placed = [equal_rows(origin_ref[side : side + 1, :][:, :slots], blocks) for side in range(2)]
    out_ref[...] = g_tile[...] + g_north[...] + g_south[...]
    for f in range(axes):
        got = jnp.zeros((blocks, halves * lanes), f32)
        for place, ref in zip(placed, (g_east, g_west)):
            data = jnp.concatenate([ref[pl.ds(f * slot_rows + h, slots, stride=halves), :] for h in range(halves)], axis=1)
            for part in split3(data):
                got = got + rows_dot(place, part, 0)
        for h in range(halves):
            at = pl.ds(f * rows + h, blocks, stride=halves)
            out_ref[at, :] = out_ref[at, :] + got[:, h * lanes : (h + 1) * lanes]


def shifted(x, axis, by):
    devices = lax.axis_size(axis)
    pairs = [(i, i + by) for i in range(devices) if 0 <= i + by < devices]
    return lax.ppermute(x, axis, pairs)


vmem = pl.BlockSpec(memory_space=pltpu.VMEM)
smem = pl.BlockSpec(memory_space=pltpu.SMEM)
in_hbm = pl.BlockSpec(memory_space=pltpu.HBM)


def sds(n):
    return jax.ShapeDtypeStruct((n, lanes), f32)


def params(mib):
    return pltpu.CompilerParams(vmem_limit_bytes=mib << 20)


def pair_scratch(total, sets):
    return [
        pltpu.VMEM((fields * total, lanes), f32),
        pltpu.VMEM((axes * total, lanes), f32),
        pltpu.VMEM((12 + halves * sets, lanes), i32),
        pltpu.SMEM((12 + halves * sets, lanes), i32),
        pltpu.SemaphoreType.DMA,
        pltpu.VMEM((halves * lanes, fields * lanes), f32),
        pltpu.VMEM((halves * lanes, fields * lanes), f32),
        pltpu.VMEM((8, halves * lanes), f32),
        pltpu.VMEM((8, halves * lanes), f32),
        pltpu.VMEM((axes * halves * lanes, lanes), f32),
        pltpu.VMEM((axes * halves * lanes, lanes), f32),
        pltpu.VMEM((axes * 8, halves * lanes), f32),
        pltpu.VMEM((axes * 8, halves * lanes), f32),
    ]


def level_call(rows, last_row, tile):
    total = 3 * rows + 8
    return pl.pallas_call(
        lambda *refs: level_kernel(rows, total, last_row, *refs),
        out_shape=sds(axes * rows),
        in_specs=[vmem],
        out_specs=vmem,
        scratch_shapes=pair_scratch(total, 1),
        compiler_params=params(24),
        name="pairs_inside",
    )(tile)


def column_call(rows, last_row, tile, north, south, g_tile):
    total = 3 * rows + 8
    return pl.pallas_call(
        lambda *refs: column_kernel(rows, total, last_row, *refs),
        out_shape=(sds(axes * rows),) * 3,
        in_specs=[vmem] * 4,
        out_specs=(vmem,) * 3,
        scratch_shapes=pair_scratch(total, 3),
        compiler_params=params(24),
        name="pairs_column",
    )(tile, north, south, g_tile)


def side_call(slots, rows, tiles, east, west, g_tiles):
    total = 3 * rows + 4 * halves * lanes + 8

    def run(*refs):
        side_kernel(slots, rows, total, refs[:3], *refs[3:5], refs[5:8], refs[8:11], *refs[11:])

    return pl.pallas_call(
        run,
        out_shape=(sds(axes * rows),) * 3 + (sds(axes * halves * slots),) * 2,
        in_specs=[vmem] * 8,
        out_specs=(vmem,) * 5,
        scratch_shapes=pair_scratch(total, 2),
        compiler_params=params(32),
        name="pairs_side",
    )(*tiles, east, west, *g_tiles)


def body(locations, solution, cotangent, block_fill, pair_own, pair_offset, pair_block, pair_count):
    points = solution.shape[2]
    slots = pair_own.shape[2]
    rows = points // lanes
    blocks = rows // halves
    own = pair_own.reshape(1, slots)
    offset = pair_offset.reshape(1, slots)
    block = pair_block.reshape(1, slots)
    count = pair_count.reshape(1, 1)
    fill = block_fill.reshape(1, blocks)
    slot_rows = fields * halves * slots + meta_rows
    last_row = lax.axis_size("ty") - 1
    note = pl.pallas_call(
        note_kernel,
        out_shape=sds(meta_rows),
        in_specs=[in_hbm] * 5,
        out_specs=vmem,
        scratch_shapes=[pltpu.SMEM((1, 1), i32), pltpu.VMEM((1, blocks), i32), pltpu.VMEM((3, 1, slots), i32),
                        pltpu.SemaphoreType.DMA((5,))],
        compiler_params=params(60),
        name="note",
    )(count, fill, own, offset, block)
    tile = jnp.concatenate([locations.reshape(axes * rows, lanes), solution.reshape(rows, lanes),
                            cotangent.reshape(rows, lanes), note], axis=0)
    north = shifted(tile, "ty", 1)
    south = shifted(tile, "ty", -1)
    to_east, to_west, origin = pl.pallas_call(
        lambda *refs: pack_kernel(slots, rows, *refs),
        out_shape=(sds(slot_rows), sds(slot_rows), jax.ShapeDtypeStruct((8, halves * lanes), f32)),
        in_specs=[vmem],
        out_specs=(vmem,) * 3,
        compiler_params=params(16),
        name="pack",
    )(tile)
    from_west = shifted(to_east, "tx", 1)
    from_east = shifted(to_west, "tx", -1)
    g_tile = level_call(rows, last_row, tile)
    g_tile, g_north, g_south = column_call(rows, last_row, tile, north, south, g_tile)
    g_north, g_tile, g_south, g_west, g_east = side_call(
        slots, rows, (north, tile, south), from_west, from_east, (g_north, g_tile, g_south))
    back_east = shifted(g_west, "tx", -1)
    back_west = shifted(g_east, "tx", 1)
    back_south = shifted(g_north, "ty", -1)
    back_north = shifted(g_south, "ty", 1)
    out = pl.pallas_call(
        lambda *refs: merge_kernel(slots, rows, *refs),
        out_shape=sds(axes * rows),
        in_specs=[vmem] * 6,
        out_specs=vmem,
        compiler_params=params(16),
        name="merge",
    )(origin, g_tile, back_north, back_south, back_east, back_west)
    return out.reshape(locations.shape)


def solution(mesh):
    placed = (
        P("ty", "tx", None, None),
        P("ty", "tx", None),
        P("ty", "tx", None),
        P("ty", "tx", None),
        P("ty", "tx", None),
        P("ty", "tx", None),
        P("ty", "tx", None),
        P("ty", "tx"),
    )
    return jax.shard_map(
        body, mesh=mesh, in_specs=placed, out_specs=P("ty", "tx", None, None), check_vma=False
    )
```

profile of v0, /device:TPU:10, one launch (start us, length us, event | category | flops | bytes accessed | tf_op | source)
XLA Modules:
  0.0 98.3 jit_solution(3903835194250561801)
XLA Ops:
  0.7 1.4 %note.1 = f32[8,128]{1,0:T(8,128)} custom-call(s32[1,1]{1,0:T(1,128)S(6)} %copy.11.count_ref, s32[1,256]{1,0:T(1,128)} %bitcast.11, s32[1,192]{1,0:T(1,128)} %bitcast.12, s32[1,192]{1,0:T(1,128)} %bitcast.13, s32[1,192]{1,0:T(1,128)} %bitcast.14), custom_call_target="tpu_custom_call" | custom-call | tf_op jit(solution)/shard_map/note/pallas_call | solution.py:523
  2.0 1.4 %pad_maximum_fusion.refs_0_.refs_1_ = f32[2568,128]{1,0:T(8,128)S(1)} fusion(f32[8,128]{1,0:T(8,128)} %note.1, f32[512,128]{1,0:T(8,128)} %bitcast.9, f32[512,128]{1,0:T(8,128)} %bitcast.10, f32[1536,128]{1,0:T(8,128)} %bitcast.8), kind=kLoop, calls=%fused_computation | loop fusion | flops 986112 | bytes 2629632 | tf_op jit(solution)/shard_map/concatenate | solution.py:533
  3.4 1.9 %collective-permute-start.1 = (f32[2568,128]{1,0:T(8,128)S(1)}, f32[2568,128]{1,0:T(8,128)S(1)}, u32[]{:S(2)}, u32[]{:S(2)}) collective-permute-start(f32[2568,128]{1,0:T(8,128)S(1)} %pad_maximum_fusion.refs_0_.refs_1_), channel_id=1, source_target_pairs={{16,0},{32,16},{48,32},{64,48},{80,64},{96,80},{112,96},{17,1},{33... | collective-permute-start | bytes 3944456 | tf_op jit(solution)/shard_map/ppermute | solution.py:434
  5.4 2.4 %collective-permute-start = (f32[2568,128]{1,0:T(8,128)S(1)}, f32[2568,128]{1,0:T(8,128)S(1)}, u32[]{:S(2)}, u32[]{:S(2)}) collective-permute-start(f32[2568,128]{1,0:T(8,128)S(1)} %pad_maximum_fusion.refs_0_.refs_1_), channel_id=1, source_target_pairs={{0,16},{16,32},{32,48},{48,64},{64,80},{80,96},{96,112},{1,17},{17... | collective-permute-start | bytes 3944456 | tf_op jit(solution)/shard_map/ppermute | solution.py:434
  7.8 1.3 %pack.1 = (f32[1928,128]{1,0:T(8,128)S(1)}, f32[1928,128]{1,0:T(8,128)S(1)}, f32[8,256]{1,0:T(8,128)S(1)}) custom-call(f32[2568,128]{1,0:T(8,128)S(1)} %pad_maximum_fusion.refs_0_.refs_1_), custom_call_target="tpu_custom_call" | custom-call | tf_op jit(solution)/shard_map/pack/pallas_call | solution.py:537
  9.1 3.8 %collective-permute-start.2 = (f32[1928,128]{1,0:T(8,128)S(1)}, f32[1928,128]{1,0:T(8,128)S(1)}, u32[]{:S(2)}, u32[]{:S(2)}) collective-permute-start(f32[1928,128]{1,0:T(8,128)S(1)} %get-tuple-element.17), channel_id=1, source_target_pairs={{0,1},{1,2},{2,3},{3,4},{4,5},{5,6},{6,7},{7,8},{8,9},{9,10},{10,1... | collective-permute-start | bytes 2961416 | tf_op jit(solution)/shard_map/ppermute | solution.py:434
  12.9 4.1 %collective-permute-start.3 = (f32[1928,128]{1,0:T(8,128)S(1)}, f32[1928,128]{1,0:T(8,128)S(1)}, u32[]{:S(2)}, u32[]{:S(2)}) collective-permute-start(f32[1928,128]{1,0:T(8,128)S(1)} %get-tuple-element.18), channel_id=1, source_target_pairs={{1,0},{2,1},{3,2},{4,3},{5,4},{6,5},{7,6},{8,7},{9,8},{10,9},{11,1... | collective-permute-start | bytes 2961416 | tf_op jit(solution)/shard_map/ppermute | solution.py:434
  17.0 6.0 %pairs_inside.1.refs_3_ = f32[1536,128]{1,0:T(8,128)S(1)} custom-call(f32[2568,128]{1,0:T(8,128)S(1)} %pad_maximum_fusion.refs_0_.refs_1_), custom_call_target="tpu_custom_call" | custom-call | tf_op jit(solution)/shard_map/pairs_inside/pallas_call | solution.py:470
  23.1 0.0 collective-permute-done.1.refs_2_
  23.1 1.3 %collective-permute-done.refs_1_.refs_0_ = f32[2568,128]{1,0:T(8,128)S(1)} collective-permute-done((f32[2568,128]{1,0:T(8,128)S(1)}, f32[2568,128]{1,0:T(8,128)S(1)}, u32[]{:S(2)}, u32[]{:S(2)}) %collective-permute-start) | collective-permute-done | bytes 1314848 | tf_op jit(solution)/shard_map/ppermute | solution.py:434
  24.3 10.8 %pairs_column.1 = (f32[1536,128]{1,0:T(8,128)S(1)}, f32[1536,128]{1,0:T(8,128)S(1)}, f32[1536,128]{1,0:T(8,128)S(1)}) custom-call(f32[2568,128]{1,0:T(8,128)S(1)} %pad_maximum_fusion.refs_0_.refs_1_, f32[2568,128]{1,0:T(8,128)S(1)} %collective-permute-done.refs_1_.refs_0_, f32[2568,128]{1,0:T(8,128)S(1)} %collective-permute-done.1.refs_2_, ...), custom_call_target="tpu_custom_call" | custom-call | tf_op jit(solution)/shard_map/pairs_column/pallas_call | solution.py:483
  35.2 2.3 %collective-permute-done.2.refs_3_ = f32[1928,128]{1,0:T(8,128)S(1)} collective-permute-done((f32[1928,128]{1,0:T(8,128)S(1)}, f32[1928,128]{1,0:T(8,128)S(1)}, u32[]{:S(2)}, u32[]{:S(2)}) %collective-permute-start.2) | collective-permute-done | bytes 987168 | tf_op jit(solution)/shard_map/ppermute | solution.py:434
  37.5 1.9 %collective-permute-done.3.refs_4_ = f32[1928,128]{1,0:T(8,128)S(1)} collective-permute-done((f32[1928,128]{1,0:T(8,128)S(1)}, f32[1928,128]{1,0:T(8,128)S(1)}, u32[]{:S(2)}, u32[]{:S(2)}) %collective-permute-start.3) | collective-permute-done | bytes 987168 | tf_op jit(solution)/shard_map/ppermute | solution.py:434
  39.4 18.3 %pairs_side.1 = (f32[1536,128]{1,0:T(8,128)S(1)}, f32[1536,128]{1,0:T(8,128)S(1)}, f32[1536,128]{1,0:T(8,128)S(1)}, f32[1152,128]{1,0:T(8,128)S(1)}, f32[1152,128]{1,0:T(8,128)S(1)}) custom-call(f32[2568,128]{1,0:T(8,128)S(1)} %collective-permute-done.refs_1_.refs_0_, f32[2568,128]{1,0:T(8,128)S(1)} %pad_maximum_fusion.refs_0_.refs_1_, ...), custom_call_target="tpu_custom_call" | custom-call | tf_op jit(solution)/shard_map/pairs_side/pallas_call | solution.py:500
  57.7 1.9 %collective-permute-start.4 = (f32[1536,128]{1,0:T(8,128)S(1)}, f32[1536,128]{1,0:T(8,128)S(1)}, u32[]{:S(2)}, u32[]{:S(2)}) collective-permute-start(f32[1536,128]{1,0:T(8,128)S(1)} %get-tuple-element.23), channel_id=1, source_target_pairs={{0,16},{16,32},{32,48},{48,64},{64,80},{80,96},{96,112},{1,17},{17... | collective-permute-start | bytes 2359304 | tf_op jit(solution)/shard_map/ppermute | solution.py:434
  59.6 3.6 %collective-permute-start.5 = (f32[1536,128]{1,0:T(8,128)S(1)}, f32[1536,128]{1,0:T(8,128)S(1)}, u32[]{:S(2)}, u32[]{:S(2)}) collective-permute-start(f32[1536,128]{1,0:T(8,128)S(1)} %get-tuple-element.24), channel_id=1, source_target_pairs={{16,0},{32,16},{48,32},{64,48},{80,64},{96,80},{112,96},{17,1},{33... | collective-permute-start | bytes 2359304 | tf_op jit(solution)/shard_map/ppermute | solution.py:434
  63.3 13.8 %collective-permute-start.6 = (f32[1152,128]{1,0:T(8,128)S(1)}, f32[1152,128]{1,0:T(8,128)S(1)}, u32[]{:S(2)}, u32[]{:S(2)}) collective-permute-start(f32[1152,128]{1,0:T(8,128)S(1)} %get-tuple-element.25), channel_id=1, source_target_pairs={{1,0},{2,1},{3,2},{4,3},{5,4},{6,5},{7,6},{8,7},{9,8},{10,9},{11,1... | collective-permute-start | bytes 1769480 | tf_op jit(solution)/shard_map/ppermute | solution.py:434
  77.1 1.9 %collective-permute-start.7 = (f32[1152,128]{1,0:T(8,128)S(1)}, f32[1152,128]{1,0:T(8,128)S(1)}, u32[]{:S(2)}, u32[]{:S(2)}) collective-permute-start(f32[1152,128]{1,0:T(8,128)S(1)} %get-tuple-element.26), channel_id=1, source_target_pairs={{0,1},{1,2},{2,3},{3,4},{4,5},{5,6},{6,7},{7,8},{8,9},{9,10},{10,1... | collective-permute-start | bytes 1769480 | tf_op jit(solution)/shard_map/ppermute | solution.py:434
  79.0 11.3 %collective-permute-done.6.refs_4_ = f32[1152,128]{1,0:T(8,128)S(1)} collective-permute-done((f32[1152,128]{1,0:T(8,128)S(1)}, f32[1152,128]{1,0:T(8,128)S(1)}, u32[]{:S(2)}, u32[]{:S(2)}) %collective-permute-start.6) | collective-permute-done | bytes 589856 | tf_op jit(solution)/shard_map/ppermute | solution.py:434
  90.3 6.2 %collective-permute-done.7.refs_5_ = f32[1152,128]{1,0:T(8,128)S(1)} collective-permute-done((f32[1152,128]{1,0:T(8,128)S(1)}, f32[1152,128]{1,0:T(8,128)S(1)}, u32[]{:S(2)}, u32[]{:S(2)}) %collective-permute-start.7) | collective-permute-done | bytes 589856 | tf_op jit(solution)/shard_map/ppermute | solution.py:434
  96.6 0.0 collective-permute-done.4.refs_2_
  96.6 0.0 collective-permute-done.5.refs_3_
  96.6 1.7 %merge.1 = f32[1536,128]{1,0:T(8,128)} custom-call(f32[8,256]{1,0:T(8,128)S(1)} %get-tuple-element.16.refs_0_, f32[1536,128]{1,0:T(8,128)S(1)} %get-tuple-element.22.refs_1_, f32[1536,128]{1,0:T(8,128)S(1)} %collective-permute-done.4.refs_2_, f32[1536,128]{1,0:T(8,128)S(1)} %collective-permute-done.5.refs_3_, ...), custom_call_target="tpu_custom_call" | custom-call | tf_op jit(solution)/shard_map/merge/pallas_call | solution.py:555
Async XLA Ops:
  3.4 19.6 %collective-permute-start.1 = (f32[2568,128]{1,0:T(8,128)S(1)}, f32[2568,128]{1,0:T(8,128)S(1)}, u32[]{:S(2)}, u32[]{:S(2)}) collective-permute-start(f32[2568,128]{1,0:T(8,128)S(1)} %pad_maximum_fusion.refs_0_.refs_1_), channel_id=1, source_target_pairs={{16,0},{32,16},{48,32},{64,48},{80,64},{96,80},{112,96},{17,1},{33... | collective-permute-start | bytes 3944456 | tf_op jit(solution)/shard_map/ppermute | solution.py:434
  5.4 19.0 %collective-permute-start = (f32[2568,128]{1,0:T(8,128)S(1)}, f32[2568,128]{1,0:T(8,128)S(1)}, u32[]{:S(2)}, u32[]{:S(2)}) collective-permute-start(f32[2568,128]{1,0:T(8,128)S(1)} %pad_maximum_fusion.refs_0_.refs_1_), channel_id=1, source_target_pairs={{0,16},{16,32},{32,48},{48,64},{64,80},{80,96},{96,112},{1,17},{17... | collective-permute-start | bytes 3944456 | tf_op jit(solution)/shard_map/ppermute | solution.py:434
  9.1 28.4 %collective-permute-start.2 = (f32[1928,128]{1,0:T(8,128)S(1)}, f32[1928,128]{1,0:T(8,128)S(1)}, u32[]{:S(2)}, u32[]{:S(2)}) collective-permute-start(f32[1928,128]{1,0:T(8,128)S(1)} %get-tuple-element.17), channel_id=1, source_target_pairs={{0,1},{1,2},{2,3},{3,4},{4,5},{5,6},{6,7},{7,8},{8,9},{9,10},{10,1... | collective-permute-start | bytes 2961416 | tf_op jit(solution)/shard_map/ppermute | solution.py:434
  12.9 26.5 %collective-permute-start.3 = (f32[1928,128]{1,0:T(8,128)S(1)}, f32[1928,128]{1,0:T(8,128)S(1)}, u32[]{:S(2)}, u32[]{:S(2)}) collective-permute-start(f32[1928,128]{1,0:T(8,128)S(1)} %get-tuple-element.18), channel_id=1, source_target_pairs={{1,0},{2,1},{3,2},{4,3},{5,4},{6,5},{7,6},{8,7},{9,8},{10,9},{11,1... | collective-permute-start | bytes 2961416 | tf_op jit(solution)/shard_map/ppermute | solution.py:434
  57.7 38.9 %collective-permute-start.4 = (f32[1536,128]{1,0:T(8,128)S(1)}, f32[1536,128]{1,0:T(8,128)S(1)}, u32[]{:S(2)}, u32[]{:S(2)}) collective-permute-start(f32[1536,128]{1,0:T(8,128)S(1)} %get-tuple-element.23), channel_id=1, source_target_pairs={{0,16},{16,32},{32,48},{48,64},{64,80},{80,96},{96,112},{1,17},{17... | collective-permute-start | bytes 2359304 | tf_op jit(solution)/shard_map/ppermute | solution.py:434
  59.6 36.9 %collective-permute-start.5 = (f32[1536,128]{1,0:T(8,128)S(1)}, f32[1536,128]{1,0:T(8,128)S(1)}, u32[]{:S(2)}, u32[]{:S(2)}) collective-permute-start(f32[1536,128]{1,0:T(8,128)S(1)} %get-tuple-element.24), channel_id=1, source_target_pairs={{16,0},{32,16},{48,32},{64,48},{80,64},{96,80},{112,96},{17,1},{33... | collective-permute-start | bytes 2359304 | tf_op jit(solution)/shard_map/ppermute | solution.py:434
  63.3 27.1 %collective-permute-start.6 = (f32[1152,128]{1,0:T(8,128)S(1)}, f32[1152,128]{1,0:T(8,128)S(1)}, u32[]{:S(2)}, u32[]{:S(2)}) collective-permute-start(f32[1152,128]{1,0:T(8,128)S(1)} %get-tuple-element.25), channel_id=1, source_target_pairs={{1,0},{2,1},{3,2},{4,3},{5,4},{6,5},{7,6},{8,7},{9,8},{10,9},{11,1... | collective-permute-start | bytes 1769480 | tf_op jit(solution)/shard_map/ppermute | solution.py:434
  77.1 19.5 %collective-permute-start.7 = (f32[1152,128]{1,0:T(8,128)S(1)}, f32[1152,128]{1,0:T(8,128)S(1)}, u32[]{:S(2)}, u32[]{:S(2)}) collective-permute-start(f32[1152,128]{1,0:T(8,128)S(1)} %get-tuple-element.26), channel_id=1, source_target_pairs={{0,1},{1,2},{2,3},{3,4},{4,5},{5,6},{6,7},{7,8},{8,9},{9,10},{10,1... | collective-permute-start | bytes 1769480 | tf_op jit(solution)/shard_map/ppermute | solution.py:434
where the time goes:
time: 99.3 us; the launch traced here: 98.3 us
  Pallas kernels  39.6 us (40%)
  starting transfers between devices  33.6 us (34%)
  waiting for transfers between devices  23 us (23%)
  other arithmetic  1.4 us (1%)
    ppermute x8, starting transfers between devices, shifted(): return lax.ppermute(x, axis, pairs)  33.6 us
    ppermute x8, waiting for transfers between devices, shifted(): return lax.ppermute(x, axis, pairs)  23 us
    pallas_call x1, Pallas kernels, side_call(): pl.pallas_call(run, out_shape=(sds(axes * rows),) * 3 + (sds(axes * halve...  18.3 us
    pallas_call x1, Pallas kernels, column_call(): pl.pallas_call(lambda *refs: column_kernel(rows, total, last_row, *refs),...  10.8 us
    pallas_call x1, Pallas kernels, level_call(): pl.pallas_call(lambda *refs: level_kernel(rows, total, last_row, *refs),...  6.03 us
  transfers between devices with their start and end apart: 8, of which 5 were waited for; matrix products, arithmetic and copies ran while one was open for 0% of the time, Pallas kernels for 18%

commit v1 on v0

--- a/solution.py
+++ b/solution.py
@@ -10,8 +10,8 @@
 fields = 5
 axes = 3
 meta_rows = 8
-kinds = 5
-kept = 32
+kinds = 4
+kept = 16
 bf16 = jnp.bfloat16
 f32 = jnp.float32
 i32 = jnp.int32
@@ -121,8 +121,8 @@
 
 
 def shape_of(kind):
-    steps = (16, 24, 16, 24, 32)[kind]
-    return steps, -(-steps // 16), (1, 1, 2, 2, 2)[kind]
+    steps = (16, 16, 24, 32)[kind]
+    return steps, -(-steps // 16), (1, 2, 2, 2)[kind]
 
 
 def pair_loops(total, spare, table, src, grad, buffers):
@@ -229,7 +229,8 @@
         @pl.when(turns > 0)
         def _(k=k, turns=turns, turn=turn):
             spread(k, 0, mixed0, partner0)
-            lax.fori_loop(0, turns, turn, 0)
+            lax.fori_loop(0, turns >> 1, lambda t, c: turn(2 * t + 1, turn(2 * t, c)), 0)
+            lax.fori_loop(turns & ~1, turns, turn, 0)
             finish(k, 2 * turns - 1, own1, far1)
 
 
@@ -238,11 +239,10 @@
     found = []
     for a, b, fill_a, fill_b, live in entries:
         size_a, size_b = (fill_a + 63) >> 6, (fill_b + 63) >> 6
-        two_a, two_b = (size_a > 2).astype(i32), (size_b > 2).astype(i32)
-        swap = (size_a * (1 + two_b) > size_b * (1 + two_a)) | ((size_a > 3) & (size_b < 3))
+        swap = size_a > size_b
         a, b = jnp.where(swap, b, a), jnp.where(swap, a, b)
         size_a, size_b = jnp.where(swap, size_b, size_a), jnp.where(swap, size_a, size_b)
-        kind = jnp.maximum(size_a - 2, 0) + jnp.where(size_b > 2, 2, 0)
+        kind = jnp.maximum(size_a - 2, 0) + jnp.where(size_b > 2, 1, 0)
         marks = [live & (kind == k) for k in range(kinds)]
         counts = running(stacked(marks, size))
         values = stacked([a & 255, a >> 8, b & 255, b >> 8], size)
@@ -268,7 +268,7 @@
     lane_id = lax.broadcasted_iota(i32, (1, lanes), 1)
     bounds = jnp.zeros((1, lanes), i32)
     firsts, totals = [f.astype(i32) for f in firsts], [t.astype(i32) for t in totals]
-    for k in (0, 2, 3):
+    for k in range(kinds - 1):
         odd = totals[k] & 1
         totals[k], firsts[k + 1], totals[k + 1] = totals[k] - odd, firsts[k + 1] - odd, totals[k + 1] + odd
     for k in range(kinds):

time: 99.3 us -> 95.3 us (0.960)
  Pallas kernels: 39.6 us -> 37.6 us
  starting transfers between devices: 33.6 us -> 31.6 us
    pallas_call x1, Pallas kernels: 6.03 us -> 3.84 us  [level_call(): pl.pallas_call(lambda *refs: level_kernel(rows, total, last_row, *refs),...]
    ppermute x8, starting transfers between devices: 33.6 us -> 31.6 us  [shifted(): return lax.ppermute(x, axis, pairs)]
    pallas_call x1, Pallas kernels: 10.8 us -> 12 us  [column_call(): pl.pallas_call(lambda *refs: column_kernel(rows, total, last_row, *refs),...]
where the time goes in v1:
time: 95.3 us; the launch traced here: 94.2 us
  Pallas kernels  37.6 us (39%)
  starting transfers between devices  31.6 us (33%)
  waiting for transfers between devices  22.8 us (24%)
  other arithmetic  1.4 us (1%)
    ppermute x8, starting transfers between devices, shifted(): return lax.ppermute(x, axis, pairs)  31.6 us
    ppermute x8, waiting for transfers between devices, shifted(): return lax.ppermute(x, axis, pairs)  22.8 us
    pallas_call x1, Pallas kernels, side_call(): pl.pallas_call(run, out_shape=(sds(axes * rows),) * 3 + (sds(axes * halve...  17.4 us
    pallas_call x1, Pallas kernels, column_call(): pl.pallas_call(lambda *refs: column_kernel(rows, total, last_row, *refs),...  12 us
    pallas_call x1, Pallas kernels, level_call(): pl.pallas_call(lambda *refs: level_kernel(rows, total, last_row, *refs),...  3.84 us
  transfers between devices with their start and end apart: 8, of which 5 were waited for; matrix products, arithmetic and copies ran while one was open for 0% of the time, Pallas kernels for 18%

profile of v1, /device:TPU:10, one launch (start us, length us, event | category | flops | bytes accessed | tf_op | source)
XLA Modules:
  0.0 94.2 jit_solution(8559973070763797523)
XLA Ops:
  0.7 1.4 %note.1 = f32[8,128]{1,0:T(8,128)} custom-call(s32[1,1]{1,0:T(1,128)S(6)} %copy.11.count_ref, s32[1,256]{1,0:T(1,128)} %bitcast.11, s32[1,192]{1,0:T(1,128)} %bitcast.12, s32[1,192]{1,0:T(1,128)} %bitcast.13, s32[1,192]{1,0:T(1,128)} %bitcast.14), custom_call_target="tpu_custom_call" | custom-call | tf_op jit(solution)/shard_map/note/pallas_call | solution.py:523
  2.0 1.4 %pad_maximum_fusion.refs_0_.refs_1_ = f32[2568,128]{1,0:T(8,128)S(1)} fusion(f32[8,128]{1,0:T(8,128)} %note.1, f32[512,128]{1,0:T(8,128)} %bitcast.9, f32[512,128]{1,0:T(8,128)} %bitcast.10, f32[1536,128]{1,0:T(8,128)} %bitcast.8), kind=kLoop, calls=%fused_computation | loop fusion | flops 986112 | bytes 2629632 | tf_op jit(solution)/shard_map/concatenate | solution.py:533
  3.4 1.9 %collective-permute-start.1 = (f32[2568,128]{1,0:T(8,128)S(1)}, f32[2568,128]{1,0:T(8,128)S(1)}, u32[]{:S(2)}, u32[]{:S(2)}) collective-permute-start(f32[2568,128]{1,0:T(8,128)S(1)} %pad_maximum_fusion.refs_0_.refs_1_), channel_id=1, source_target_pairs={{16,0},{32,16},{48,32},{64,48},{80,64},{96,80},{112,96},{17,1},{33... | collective-permute-start | bytes 3944456 | tf_op jit(solution)/shard_map/ppermute | solution.py:434
  5.4 2.4 %collective-permute-start = (f32[2568,128]{1,0:T(8,128)S(1)}, f32[2568,128]{1,0:T(8,128)S(1)}, u32[]{:S(2)}, u32[]{:S(2)}) collective-permute-start(f32[2568,128]{1,0:T(8,128)S(1)} %pad_maximum_fusion.refs_0_.refs_1_), channel_id=1, source_target_pairs={{0,16},{16,32},{32,48},{48,64},{64,80},{80,96},{96,112},{1,17},{17... | collective-permute-start | bytes 3944456 | tf_op jit(solution)/shard_map/ppermute | solution.py:434
  7.8 1.3 %pack.1 = (f32[1928,128]{1,0:T(8,128)S(1)}, f32[1928,128]{1,0:T(8,128)S(1)}, f32[8,256]{1,0:T(8,128)S(1)}) custom-call(f32[2568,128]{1,0:T(8,128)S(1)} %pad_maximum_fusion.refs_0_.refs_1_), custom_call_target="tpu_custom_call" | custom-call | tf_op jit(solution)/shard_map/pack/pallas_call | solution.py:537
  9.1 3.8 %collective-permute-start.2 = (f32[1928,128]{1,0:T(8,128)S(1)}, f32[1928,128]{1,0:T(8,128)S(1)}, u32[]{:S(2)}, u32[]{:S(2)}) collective-permute-start(f32[1928,128]{1,0:T(8,128)S(1)} %get-tuple-element.17), channel_id=1, source_target_pairs={{0,1},{1,2},{2,3},{3,4},{4,5},{5,6},{6,7},{7,8},{8,9},{9,10},{10,1... | collective-permute-start | bytes 2961416 | tf_op jit(solution)/shard_map/ppermute | solution.py:434
  12.9 4.1 %collective-permute-start.3 = (f32[1928,128]{1,0:T(8,128)S(1)}, f32[1928,128]{1,0:T(8,128)S(1)}, u32[]{:S(2)}, u32[]{:S(2)}) collective-permute-start(f32[1928,128]{1,0:T(8,128)S(1)} %get-tuple-element.18), channel_id=1, source_target_pairs={{1,0},{2,1},{3,2},{4,3},{5,4},{6,5},{7,6},{8,7},{9,8},{10,9},{11,1... | collective-permute-start | bytes 2961416 | tf_op jit(solution)/shard_map/ppermute | solution.py:434
  17.0 3.8 %pairs_inside.1.refs_3_ = f32[1536,128]{1,0:T(8,128)S(1)} custom-call(f32[2568,128]{1,0:T(8,128)S(1)} %pad_maximum_fusion.refs_0_.refs_1_), custom_call_target="tpu_custom_call" | custom-call | tf_op jit(solution)/shard_map/pairs_inside/pallas_call | solution.py:470
  20.9 0.0 collective-permute-done.1.refs_2_
  20.9 3.5 %collective-permute-done.refs_1_.refs_0_ = f32[2568,128]{1,0:T(8,128)S(1)} collective-permute-done((f32[2568,128]{1,0:T(8,128)S(1)}, f32[2568,128]{1,0:T(8,128)S(1)}, u32[]{:S(2)}, u32[]{:S(2)}) %collective-permute-start) | collective-permute-done | bytes 1314848 | tf_op jit(solution)/shard_map/ppermute | solution.py:434
  24.3 12.0 %pairs_column.1 = (f32[1536,128]{1,0:T(8,128)S(1)}, f32[1536,128]{1,0:T(8,128)S(1)}, f32[1536,128]{1,0:T(8,128)S(1)}) custom-call(f32[2568,128]{1,0:T(8,128)S(1)} %pad_maximum_fusion.refs_0_.refs_1_, f32[2568,128]{1,0:T(8,128)S(1)} %collective-permute-done.refs_1_.refs_0_, f32[2568,128]{1,0:T(8,128)S(1)} %collective-permute-done.1.refs_2_, ...), custom_call_target="tpu_custom_call" | custom-call | tf_op jit(solution)/shard_map/pairs_column/pallas_call | solution.py:483
  36.3 1.1 %collective-permute-done.2.refs_3_ = f32[1928,128]{1,0:T(8,128)S(1)} collective-permute-done((f32[1928,128]{1,0:T(8,128)S(1)}, f32[1928,128]{1,0:T(8,128)S(1)}, u32[]{:S(2)}, u32[]{:S(2)}) %collective-permute-start.2) | collective-permute-done | bytes 987168 | tf_op jit(solution)/shard_map/ppermute | solution.py:434
  37.5 1.9 %collective-permute-done.3.refs_4_ = f32[1928,128]{1,0:T(8,128)S(1)} collective-permute-done((f32[1928,128]{1,0:T(8,128)S(1)}, f32[1928,128]{1,0:T(8,128)S(1)}, u32[]{:S(2)}, u32[]{:S(2)}) %collective-permute-start.3) | collective-permute-done | bytes 987168 | tf_op jit(solution)/shard_map/ppermute | solution.py:434
  39.4 17.4 %pairs_side.1 = (f32[1536,128]{1,0:T(8,128)S(1)}, f32[1536,128]{1,0:T(8,128)S(1)}, f32[1536,128]{1,0:T(8,128)S(1)}, f32[1152,128]{1,0:T(8,128)S(1)}, f32[1152,128]{1,0:T(8,128)S(1)}) custom-call(f32[2568,128]{1,0:T(8,128)S(1)} %collective-permute-done.refs_1_.refs_0_, f32[2568,128]{1,0:T(8,128)S(1)} %pad_maximum_fusion.refs_0_.refs_1_, ...), custom_call_target="tpu_custom_call" | custom-call | tf_op jit(solution)/shard_map/pairs_side/pallas_call | solution.py:500
  56.8 1.9 %collective-permute-start.4 = (f32[1536,128]{1,0:T(8,128)S(1)}, f32[1536,128]{1,0:T(8,128)S(1)}, u32[]{:S(2)}, u32[]{:S(2)}) collective-permute-start(f32[1536,128]{1,0:T(8,128)S(1)} %get-tuple-element.23), channel_id=1, source_target_pairs={{0,16},{16,32},{32,48},{48,64},{64,80},{80,96},{96,112},{1,17},{17... | collective-permute-start | bytes 2359304 | tf_op jit(solution)/shard_map/ppermute | solution.py:434
  58.7 3.6 %collective-permute-start.5 = (f32[1536,128]{1,0:T(8,128)S(1)}, f32[1536,128]{1,0:T(8,128)S(1)}, u32[]{:S(2)}, u32[]{:S(2)}) collective-permute-start(f32[1536,128]{1,0:T(8,128)S(1)} %get-tuple-element.24), channel_id=1, source_target_pairs={{16,0},{32,16},{48,32},{64,48},{80,64},{96,80},{112,96},{17,1},{33... | collective-permute-start | bytes 2359304 | tf_op jit(solution)/shard_map/ppermute | solution.py:434
  62.4 11.9 %collective-permute-start.6 = (f32[1152,128]{1,0:T(8,128)S(1)}, f32[1152,128]{1,0:T(8,128)S(1)}, u32[]{:S(2)}, u32[]{:S(2)}) collective-permute-start(f32[1152,128]{1,0:T(8,128)S(1)} %get-tuple-element.25), channel_id=1, source_target_pairs={{1,0},{2,1},{3,2},{4,3},{5,4},{6,5},{7,6},{8,7},{9,8},{10,9},{11,1... | collective-permute-start | bytes 1769480 | tf_op jit(solution)/shard_map/ppermute | solution.py:434
  74.2 1.9 %collective-permute-start.7 = (f32[1152,128]{1,0:T(8,128)S(1)}, f32[1152,128]{1,0:T(8,128)S(1)}, u32[]{:S(2)}, u32[]{:S(2)}) collective-permute-start(f32[1152,128]{1,0:T(8,128)S(1)} %get-tuple-element.26), channel_id=1, source_target_pairs={{0,1},{1,2},{2,3},{3,4},{4,5},{5,6},{6,7},{7,8},{8,9},{9,10},{10,1... | collective-permute-start | bytes 1769480 | tf_op jit(solution)/shard_map/ppermute | solution.py:434
  76.2 9.6 %collective-permute-done.6.refs_4_ = f32[1152,128]{1,0:T(8,128)S(1)} collective-permute-done((f32[1152,128]{1,0:T(8,128)S(1)}, f32[1152,128]{1,0:T(8,128)S(1)}, u32[]{:S(2)}, u32[]{:S(2)}) %collective-permute-start.6) | collective-permute-done | bytes 589856 | tf_op jit(solution)/shard_map/ppermute | solution.py:434
  85.8 6.7 %collective-permute-done.7.refs_5_ = f32[1152,128]{1,0:T(8,128)S(1)} collective-permute-done((f32[1152,128]{1,0:T(8,128)S(1)}, f32[1152,128]{1,0:T(8,128)S(1)}, u32[]{:S(2)}, u32[]{:S(2)}) %collective-permute-start.7) | collective-permute-done | bytes 589856 | tf_op jit(solution)/shard_map/ppermute | solution.py:434
  92.4 0.0 collective-permute-done.4.refs_2_
  92.4 0.0 collective-permute-done.5.refs_3_
  92.5 1.7 %merge.1 = f32[1536,128]{1,0:T(8,128)} custom-call(f32[8,256]{1,0:T(8,128)S(1)} %get-tuple-element.16.refs_0_, f32[1536,128]{1,0:T(8,128)S(1)} %get-tuple-element.22.refs_1_, f32[1536,128]{1,0:T(8,128)S(1)} %collective-permute-done.4.refs_2_, f32[1536,128]{1,0:T(8,128)S(1)} %collective-permute-done.5.refs_3_, ...), custom_call_target="tpu_custom_call" | custom-call | tf_op jit(solution)/shard_map/merge/pallas_call | solution.py:555
Async XLA Ops:
  3.4 17.4 %collective-permute-start.1 = (f32[2568,128]{1,0:T(8,128)S(1)}, f32[2568,128]{1,0:T(8,128)S(1)}, u32[]{:S(2)}, u32[]{:S(2)}) collective-permute-start(f32[2568,128]{1,0:T(8,128)S(1)} %pad_maximum_fusion.refs_0_.refs_1_), channel_id=1, source_target_pairs={{16,0},{32,16},{48,32},{64,48},{80,64},{96,80},{112,96},{17,1},{33... | collective-permute-start | bytes 3944456 | tf_op jit(solution)/shard_map/ppermute | solution.py:434
  5.4 19.0 %collective-permute-start = (f32[2568,128]{1,0:T(8,128)S(1)}, f32[2568,128]{1,0:T(8,128)S(1)}, u32[]{:S(2)}, u32[]{:S(2)}) collective-permute-start(f32[2568,128]{1,0:T(8,128)S(1)} %pad_maximum_fusion.refs_0_.refs_1_), channel_id=1, source_target_pairs={{0,16},{16,32},{32,48},{48,64},{64,80},{80,96},{96,112},{1,17},{17... | collective-permute-start | bytes 3944456 | tf_op jit(solution)/shard_map/ppermute | solution.py:434
  9.1 28.4 %collective-permute-start.2 = (f32[1928,128]{1,0:T(8,128)S(1)}, f32[1928,128]{1,0:T(8,128)S(1)}, u32[]{:S(2)}, u32[]{:S(2)}) collective-permute-start(f32[1928,128]{1,0:T(8,128)S(1)} %get-tuple-element.17), channel_id=1, source_target_pairs={{0,1},{1,2},{2,3},{3,4},{4,5},{5,6},{6,7},{7,8},{8,9},{9,10},{10,1... | collective-permute-start | bytes 2961416 | tf_op jit(solution)/shard_map/ppermute | solution.py:434
  12.9 26.5 %collective-permute-start.3 = (f32[1928,128]{1,0:T(8,128)S(1)}, f32[1928,128]{1,0:T(8,128)S(1)}, u32[]{:S(2)}, u32[]{:S(2)}) collective-permute-start(f32[1928,128]{1,0:T(8,128)S(1)} %get-tuple-element.18), channel_id=1, source_target_pairs={{1,0},{2,1},{3,2},{4,3},{5,4},{6,5},{7,6},{8,7},{9,8},{10,9},{11,1... | collective-permute-start | bytes 2961416 | tf_op jit(solution)/shard_map/ppermute | solution.py:434
  56.8 35.7 %collective-permute-start.4 = (f32[1536,128]{1,0:T(8,128)S(1)}, f32[1536,128]{1,0:T(8,128)S(1)}, u32[]{:S(2)}, u32[]{:S(2)}) collective-permute-start(f32[1536,128]{1,0:T(8,128)S(1)} %get-tuple-element.23), channel_id=1, source_target_pairs={{0,16},{16,32},{32,48},{48,64},{64,80},{80,96},{96,112},{1,17},{17... | collective-permute-start | bytes 2359304 | tf_op jit(solution)/shard_map/ppermute | solution.py:434
  58.7 33.7 %collective-permute-start.5 = (f32[1536,128]{1,0:T(8,128)S(1)}, f32[1536,128]{1,0:T(8,128)S(1)}, u32[]{:S(2)}, u32[]{:S(2)}) collective-permute-start(f32[1536,128]{1,0:T(8,128)S(1)} %get-tuple-element.24), channel_id=1, source_target_pairs={{16,0},{32,16},{48,32},{64,48},{80,64},{96,80},{112,96},{17,1},{33... | collective-permute-start | bytes 2359304 | tf_op jit(solution)/shard_map/ppermute | solution.py:434
  62.4 23.4 %collective-permute-start.6 = (f32[1152,128]{1,0:T(8,128)S(1)}, f32[1152,128]{1,0:T(8,128)S(1)}, u32[]{:S(2)}, u32[]{:S(2)}) collective-permute-start(f32[1152,128]{1,0:T(8,128)S(1)} %get-tuple-element.25), channel_id=1, source_target_pairs={{1,0},{2,1},{3,2},{4,3},{5,4},{6,5},{7,6},{8,7},{9,8},{10,9},{11,1... | collective-permute-start | bytes 1769480 | tf_op jit(solution)/shard_map/ppermute | solution.py:434
  74.2 18.2 %collective-permute-start.7 = (f32[1152,128]{1,0:T(8,128)S(1)}, f32[1152,128]{1,0:T(8,128)S(1)}, u32[]{:S(2)}, u32[]{:S(2)}) collective-permute-start(f32[1152,128]{1,0:T(8,128)S(1)} %get-tuple-element.26), channel_id=1, source_target_pairs={{0,1},{1,2},{2,3},{3,4},{4,5},{5,6},{6,7},{7,8},{8,9},{9,10},{10,1... | collective-permute-start | bytes 1769480 | tf_op jit(solution)/shard_map/ppermute | solution.py:434

commit v2 on v1

--- a/solution.py
+++ b/solution.py
@@ -404,19 +404,23 @@
             grad[f * total + base : f * total + base + slot_rows, :] = jnp.zeros((slot_rows, lanes), f32)
     copy.wait()
     pair_loops(total, 10 * lanes, table, src, grad, buffers)
-    for ref, base in zip(o_tiles, bases):
+    outs = (o_tiles[:2], o_tiles[2:3], o_tiles[3:])
+    for refs, base in zip(outs, bases):
         for f in range(axes):
-            ref[f * rows : (f + 1) * rows, :] = grad[f * total + base : f * total + base + rows, :]
+            ref, at = (refs[1], 0) if len(refs) > 1 and f == axes - 1 else (refs[0], f)
+            ref[at * rows : (at + 1) * rows, :] = grad[f * total + base : f * total + base + rows, :]
     for ref, (_, base) in zip((o_east, o_west), slot_places):
         for f in range(axes):
             ref[f * slot_rows : (f + 1) * slot_rows, :] = grad[f * total + base : f * total + base + slot_rows, :]
 
 
-def merge_kernel(slots, rows, origin_ref, g_tile, g_north, g_south, g_east, g_west, out_ref):
+def merge_kernel(slots, rows, origin_ref, g_tile, g_north, g_north_z, g_south, g_south_z, g_east, g_west, out_ref):
     blocks = rows // halves
     slot_rows = halves * slots
     placed = [equal_rows(origin_ref[side : side + 1, :][:, :slots], blocks) for side in range(2)]
-    out_ref[...] = g_tile[...] + g_north[...] + g_south[...]
+    plane = (axes - 1) * rows
+    out_ref[:plane, :] = g_tile[:plane, :] + g_north[...] + g_south[...]
+    out_ref[plane:, :] = g_tile[plane:, :] + g_north_z[...] + g_south_z[...]
     for f in range(axes):
         got = jnp.zeros((blocks, halves * lanes), f32)
         for place, ref in zip(placed, (g_east, g_west)):
@@ -495,13 +499,14 @@
     total = 3 * rows + 4 * halves * lanes + 8
 
     def run(*refs):
-        side_kernel(slots, rows, total, refs[:3], *refs[3:5], refs[5:8], refs[8:11], *refs[11:])
+        side_kernel(slots, rows, total, refs[:3], *refs[3:5], refs[5:8], refs[8:13], *refs[13:])
 
     return pl.pallas_call(
         run,
-        out_shape=(sds(axes * rows),) * 3 + (sds(axes * halves * slots),) * 2,
+        out_shape=(sds((axes - 1) * rows), sds(rows), sds(axes * rows), sds((axes - 1) * rows), sds(rows))
+        + (sds(axes * halves * slots),) * 2,
         in_specs=[vmem] * 8,
-        out_specs=(vmem,) * 5,
+        out_specs=(vmem,) * 7,
         scratch_shapes=pair_scratch(total, 2),
         compiler_params=params(32),
         name="pairs_side",
@@ -546,20 +551,20 @@
     from_east = shifted(to_west, "tx", -1)
     g_tile = level_call(rows, last_row, tile)
     g_tile, g_north, g_south = column_call(rows, last_row, tile, north, south, g_tile)
-    g_north, g_tile, g_south, g_west, g_east = side_call(
+    *g_north, g_tile, g_south, g_south_z, g_west, g_east = side_call(
         slots, rows, (north, tile, south), from_west, from_east, (g_north, g_tile, g_south))
     back_east = shifted(g_west, "tx", -1)
     back_west = shifted(g_east, "tx", 1)
-    back_south = shifted(g_north, "ty", -1)
-    back_north = shifted(g_south, "ty", 1)
+    back_south = [shifted(g, "ty", -1) for g in g_north]
+    back_north = [shifted(g, "ty", 1) for g in (g_south, g_south_z)]
     out = pl.pallas_call(
         lambda *refs: merge_kernel(slots, rows, *refs),
         out_shape=sds(axes * rows),
-        in_specs=[vmem] * 6,
+        in_specs=[vmem] * 8,
         out_specs=vmem,
         compiler_params=params(16),
         name="merge",
-    )(origin, g_tile, back_north, back_south, back_east, back_west)
+    )(origin, g_tile, *back_north, *back_south, back_east, back_west)
     return out.reshape(locations.shape)
 
 

time: 95.3 us -> 93.3 us (0.979)
  the two profiles are of different devices: /device:TPU:10 before, /device:TPU:7 now
where the time goes in v2:
time: 93.3 us; the launch traced here: 93.4 us
  Pallas kernels  45.1 us (48%)
  starting transfers between devices  29.9 us (32%)
  waiting for transfers between devices  16.2 us (17%)
  other arithmetic  1.4 us (2%)
    ppermute x10, starting transfers between devices, shifted(): return lax.ppermute(x, axis, pairs)  29.9 us
    pallas_call x1, Pallas kernels, side_call(): pl.pallas_call(run, out_shape=(sds((axes - 1) * rows), sds(rows), sds(axe...  26 us
    ppermute x10, waiting for transfers between devices, shifted(): return lax.ppermute(x, axis, pairs)  16.2 us
    pallas_call x1, Pallas kernels, column_call(): pl.pallas_call(lambda *refs: column_kernel(rows, total, last_row, *refs),...  9.38 us
    pallas_call x1, Pallas kernels, level_call(): pl.pallas_call(lambda *refs: level_kernel(rows, total, last_row, *refs),...  5.39 us
  transfers between devices with their start and end apart: 10, of which 3 were waited for; matrix products, arithmetic and copies ran while one was open for 0% of the time, Pallas kernels for 17%

profile of v2, /device:TPU:7, one launch (start us, length us, event | category | flops | bytes accessed | tf_op | source)
XLA Modules:
  0.0 93.4 jit_solution(11850416487732138384)
XLA Ops:
  0.7 1.4 %note.1 = f32[8,128]{1,0:T(8,128)} custom-call(s32[1,1]{1,0:T(1,128)S(6)} %copy.11.count_ref, s32[1,256]{1,0:T(1,128)} %bitcast.11, s32[1,192]{1,0:T(1,128)} %bitcast.12, s32[1,192]{1,0:T(1,128)} %bitcast.13, s32[1,192]{1,0:T(1,128)} %bitcast.14), custom_call_target="tpu_custom_call" | custom-call | tf_op jit(solution)/shard_map/note/pallas_call | solution.py:528
  2.0 1.4 %pad_maximum_fusion.refs_0_.refs_1_ = f32[2568,128]{1,0:T(8,128)S(1)} fusion(f32[8,128]{1,0:T(8,128)} %note.1, f32[512,128]{1,0:T(8,128)} %bitcast.9, f32[512,128]{1,0:T(8,128)} %bitcast.10, f32[1536,128]{1,0:T(8,128)} %bitcast.8), kind=kLoop, calls=%fused_computation | loop fusion | flops 986112 | bytes 2629632 | tf_op jit(solution)/shard_map/concatenate | solution.py:538
  3.4 2.6 %collective-permute-start.1 = (f32[2568,128]{1,0:T(8,128)S(1)}, f32[2568,128]{1,0:T(8,128)S(1)}, u32[]{:S(2)}, u32[]{:S(2)}) collective-permute-start(f32[2568,128]{1,0:T(8,128)S(1)} %pad_maximum_fusion.refs_0_.refs_1_), channel_id=1, source_target_pairs={{16,0},{32,16},{48,32},{64,48},{80,64},{96,80},{112,96},{17,1},{33... | collective-permute-start | bytes 3944456 | tf_op jit(solution)/shard_map/ppermute | solution.py:438
  6.0 3.1 %collective-permute-start = (f32[2568,128]{1,0:T(8,128)S(1)}, f32[2568,128]{1,0:T(8,128)S(1)}, u32[]{:S(2)}, u32[]{:S(2)}) collective-permute-start(f32[2568,128]{1,0:T(8,128)S(1)} %pad_maximum_fusion.refs_0_.refs_1_), channel_id=1, source_target_pairs={{0,16},{16,32},{32,48},{48,64},{64,80},{80,96},{96,112},{1,17},{17... | collective-permute-start | bytes 3944456 | tf_op jit(solution)/shard_map/ppermute | solution.py:438
  9.1 1.3 %pack.1 = (f32[1928,128]{1,0:T(8,128)S(1)}, f32[1928,128]{1,0:T(8,128)S(1)}, f32[8,256]{1,0:T(8,128)S(1)}) custom-call(f32[2568,128]{1,0:T(8,128)S(1)} %pad_maximum_fusion.refs_0_.refs_1_), custom_call_target="tpu_custom_call" | custom-call | tf_op jit(solution)/shard_map/pack/pallas_call | solution.py:542
  10.4 3.5 %collective-permute-start.2 = (f32[1928,128]{1,0:T(8,128)S(1)}, f32[1928,128]{1,0:T(8,128)S(1)}, u32[]{:S(2)}, u32[]{:S(2)}) collective-permute-start(f32[1928,128]{1,0:T(8,128)S(1)} %get-tuple-element.19), channel_id=1, source_target_pairs={{0,1},{1,2},{2,3},{3,4},{4,5},{5,6},{6,7},{7,8},{8,9},{9,10},{10,1... | collective-permute-start | bytes 2961416 | tf_op jit(solution)/shard_map/ppermute | solution.py:438
  14.0 4.3 %collective-permute-start.3 = (f32[1928,128]{1,0:T(8,128)S(1)}, f32[1928,128]{1,0:T(8,128)S(1)}, u32[]{:S(2)}, u32[]{:S(2)}) collective-permute-start(f32[1928,128]{1,0:T(8,128)S(1)} %get-tuple-element.20), channel_id=1, source_target_pairs={{1,0},{2,1},{3,2},{4,3},{5,4},{6,5},{7,6},{8,7},{9,8},{10,9},{11,1... | collective-permute-start | bytes 2961416 | tf_op jit(solution)/shard_map/ppermute | solution.py:438
  18.3 5.4 %pairs_inside.1.refs_3_ = f32[1536,128]{1,0:T(8,128)S(1)} custom-call(f32[2568,128]{1,0:T(8,128)S(1)} %pad_maximum_fusion.refs_0_.refs_1_), custom_call_target="tpu_custom_call" | custom-call | tf_op jit(solution)/shard_map/pairs_inside/pallas_call | solution.py:474
  23.7 0.0 collective-permute-done.1.refs_2_
  23.7 0.0 collective-permute-done.refs_1_.refs_0_
  23.7 9.4 %pairs_column.1 = (f32[1536,128]{1,0:T(8,128)S(1)}, f32[1536,128]{1,0:T(8,128)S(1)}, f32[1536,128]{1,0:T(8,128)S(1)}) custom-call(f32[2568,128]{1,0:T(8,128)S(1)} %pad_maximum_fusion.refs_0_.refs_1_, f32[2568,128]{1,0:T(8,128)S(1)} %collective-permute-done.refs_1_.refs_0_, f32[2568,128]{1,0:T(8,128)S(1)} %collective-permute-done.1.refs_2_, ...), custom_call_target="tpu_custom_call" | custom-call | tf_op jit(solution)/shard_map/pairs_column/pallas_call | solution.py:487
  33.1 4.9 %collective-permute-done.2.refs_3_ = f32[1928,128]{1,0:T(8,128)S(1)} collective-permute-done((f32[1928,128]{1,0:T(8,128)S(1)}, f32[1928,128]{1,0:T(8,128)S(1)}, u32[]{:S(2)}, u32[]{:S(2)}) %collective-permute-start.2) | collective-permute-done | bytes 987168 | tf_op jit(solution)/shard_map/ppermute | solution.py:438
  38.0 1.8 %collective-permute-done.3.refs_4_ = f32[1928,128]{1,0:T(8,128)S(1)} collective-permute-done((f32[1928,128]{1,0:T(8,128)S(1)}, f32[1928,128]{1,0:T(8,128)S(1)}, u32[]{:S(2)}, u32[]{:S(2)}) %collective-permute-start.3) | collective-permute-done | bytes 987168 | tf_op jit(solution)/shard_map/ppermute | solution.py:438
  39.8 26.0 %pairs_side.1 = (f32[1024,128]{1,0:T(8,128)S(1)}, f32[512,128]{1,0:T(8,128)S(1)}, f32[1536,128]{1,0:T(8,128)S(1)}, f32[1024,128]{1,0:T(8,128)S(1)}, f32[512,128]...) custom-call(f32[2568,128]{1,0:T(8,128)S(1)} %collective-permute-done.refs_1_.refs_0_, ...), custom_call_target="tpu_custom_call" | custom-call | tf_op jit(solution)/shard_map/pairs_side/pallas_call | solution.py:504
  65.8 1.9 %collective-permute-start.8 = (f32[1152,128]{1,0:T(8,128)S(1)}, f32[1152,128]{1,0:T(8,128)S(1)}, u32[]{:S(2)}, u32[]{:S(2)}) collective-permute-start(f32[1152,128]{1,0:T(8,128)S(1)} %get-tuple-element.29), channel_id=1, source_target_pairs={{1,0},{2,1},{3,2},{4,3},{5,4},{6,5},{7,6},{8,7},{9,8},{10,9},{11,1... | collective-permute-start | bytes 1769480 | tf_op jit(solution)/shard_map/ppermute | solution.py:438
  67.8 3.4 %collective-permute-start.9 = (f32[1152,128]{1,0:T(8,128)S(1)}, f32[1152,128]{1,0:T(8,128)S(1)}, u32[]{:S(2)}, u32[]{:S(2)}) collective-permute-start(f32[1152,128]{1,0:T(8,128)S(1)} %get-tuple-element.30), channel_id=1, source_target_pairs={{0,1},{1,2},{2,3},{3,4},{4,5},{5,6},{6,7},{7,8},{8,9},{9,10},{10,1... | collective-permute-start | bytes 1769480 | tf_op jit(solution)/shard_map/ppermute | solution.py:438
  71.1 1.9 %collective-permute-start.5 = (f32[512,128]{1,0:T(8,128)S(1)}, f32[512,128]{1,0:T(8,128)S(1)}, u32[]{:S(2)}, u32[]{:S(2)}) collective-permute-start(f32[512,128]{1,0:T(8,128)S(1)} %get-tuple-element.26), channel_id=1, source_target_pairs={{0,16},{16,32},{32,48},{48,64},{64,80},{80,96},{96,112},{1,17},{17... | collective-permute-start | bytes 786440 | tf_op jit(solution)/shard_map/ppermute | solution.py:438
  73.1 5.3 %collective-permute-start.4 = (f32[1024,128]{1,0:T(8,128)S(1)}, f32[1024,128]{1,0:T(8,128)S(1)}, u32[]{:S(2)}, u32[]{:S(2)}) collective-permute-start(f32[1024,128]{1,0:T(8,128)S(1)} %get-tuple-element.25), channel_id=1, source_target_pairs={{0,16},{16,32},{32,48},{48,64},{64,80},{80,96},{96,112},{1,17},{17... | collective-permute-start | bytes 1572872 | tf_op jit(solution)/shard_map/ppermute | solution.py:438
  78.4 1.9 %collective-permute-start.6 = (f32[1024,128]{1,0:T(8,128)S(1)}, f32[1024,128]{1,0:T(8,128)S(1)}, u32[]{:S(2)}, u32[]{:S(2)}) collective-permute-start(f32[1024,128]{1,0:T(8,128)S(1)} %get-tuple-element.27), channel_id=1, source_target_pairs={{16,0},{32,16},{48,32},{64,48},{80,64},{96,80},{112,96},{17,1},{33... | collective-permute-start | bytes 1572872 | tf_op jit(solution)/shard_map/ppermute | solution.py:438
  80.3 0.0 collective-permute-done.5.refs_3_
  80.3 1.9 %collective-permute-start.7 = (f32[512,128]{1,0:T(8,128)S(1)}, f32[512,128]{1,0:T(8,128)S(1)}, u32[]{:S(2)}, u32[]{:S(2)}) collective-permute-start(f32[512,128]{1,0:T(8,128)S(1)} %get-tuple-element.28), channel_id=1, source_target_pairs={{16,0},{32,16},{48,32},{64,48},{80,64},{96,80},{112,96},{17,1},{33... | collective-permute-start | bytes 786440 | tf_op jit(solution)/shard_map/ppermute | solution.py:438
  82.2 9.4 %collective-permute-done.7.refs_5_ = f32[512,128]{1,0:T(8,128)S(1)} collective-permute-done((f32[512,128]{1,0:T(8,128)S(1)}, f32[512,128]{1,0:T(8,128)S(1)}, u32[]{:S(2)}, u32[]{:S(2)}) %collective-permute-start.7) | collective-permute-done | bytes 262176 | tf_op jit(solution)/shard_map/ppermute | solution.py:438
  91.7 0.0 collective-permute-done.4.refs_2_
  91.7 0.0 collective-permute-done.6.refs_4_
  91.7 0.0 collective-permute-done.8.refs_6_
  91.7 0.0 collective-permute-done.9.refs_7_
  91.7 1.7 %merge.1 = f32[1536,128]{1,0:T(8,128)} custom-call(f32[8,256]{1,0:T(8,128)S(1)} %get-tuple-element.18.refs_0_, f32[1536,128]{1,0:T(8,128)S(1)} %get-tuple-element.24.refs_1_, f32[1024,128]{1,0:T(8,128)S(1)} %collective-permute-done.4.refs_2_, f32[512,128]{1,0:T(8,128)S(1)} %collective-permute-done.5.refs_3_, f32[1024,128]{1,0:T(8,128)S(1)} %collective-permute-done.6.refs_4_, ...), custom_call_target="tpu_custom_call" | custom-call | tf_op jit(solution)/shard_map/merge/pallas_call | solution.py:560
Async XLA Ops:
  3.4 20.2 %collective-permute-start.1 = (f32[2568,128]{1,0:T(8,128)S(1)}, f32[2568,128]{1,0:T(8,128)S(1)}, u32[]{:S(2)}, u32[]{:S(2)}) collective-permute-start(f32[2568,128]{1,0:T(8,128)S(1)} %pad_maximum_fusion.refs_0_.refs_1_), channel_id=1, source_target_pairs={{16,0},{32,16},{48,32},{64,48},{80,64},{96,80},{112,96},{17,1},{33... | collective-permute-start | bytes 3944456 | tf_op jit(solution)/shard_map/ppermute | solution.py:438
  6.0 17.7 %collective-permute-start = (f32[2568,128]{1,0:T(8,128)S(1)}, f32[2568,128]{1,0:T(8,128)S(1)}, u32[]{:S(2)}, u32[]{:S(2)}) collective-permute-start(f32[2568,128]{1,0:T(8,128)S(1)} %pad_maximum_fusion.refs_0_.refs_1_), channel_id=1, source_target_pairs={{0,16},{16,32},{32,48},{48,64},{64,80},{80,96},{96,112},{1,17},{17... | collective-permute-start | bytes 3944456 | tf_op jit(solution)/shard_map/ppermute | solution.py:438
  10.4 27.6 %collective-permute-start.2 = (f32[1928,128]{1,0:T(8,128)S(1)}, f32[1928,128]{1,0:T(8,128)S(1)}, u32[]{:S(2)}, u32[]{:S(2)}) collective-permute-start(f32[1928,128]{1,0:T(8,128)S(1)} %get-tuple-element.19), channel_id=1, source_target_pairs={{0,1},{1,2},{2,3},{3,4},{4,5},{5,6},{6,7},{7,8},{8,9},{9,10},{10,1... | collective-permute-start | bytes 2961416 | tf_op jit(solution)/shard_map/ppermute | solution.py:438
  14.0 25.9 %collective-permute-start.3 = (f32[1928,128]{1,0:T(8,128)S(1)}, f32[1928,128]{1,0:T(8,128)S(1)}, u32[]{:S(2)}, u32[]{:S(2)}) collective-permute-start(f32[1928,128]{1,0:T(8,128)S(1)} %get-tuple-element.20), channel_id=1, source_target_pairs={{1,0},{2,1},{3,2},{4,3},{5,4},{6,5},{7,6},{8,7},{9,8},{10,9},{11,1... | collective-permute-start | bytes 2961416 | tf_op jit(solution)/shard_map/ppermute | solution.py:438
  65.8 25.9 %collective-permute-start.8 = (f32[1152,128]{1,0:T(8,128)S(1)}, f32[1152,128]{1,0:T(8,128)S(1)}, u32[]{:S(2)}, u32[]{:S(2)}) collective-permute-start(f32[1152,128]{1,0:T(8,128)S(1)} %get-tuple-element.29), channel_id=1, source_target_pairs={{1,0},{2,1},{3,2},{4,3},{5,4},{6,5},{7,6},{8,7},{9,8},{10,9},{11,1... | collective-permute-start | bytes 1769480 | tf_op jit(solution)/shard_map/ppermute | solution.py:438
  67.8 23.9 %collective-permute-start.9 = (f32[1152,128]{1,0:T(8,128)S(1)}, f32[1152,128]{1,0:T(8,128)S(1)}, u32[]{:S(2)}, u32[]{:S(2)}) collective-permute-start(f32[1152,128]{1,0:T(8,128)S(1)} %get-tuple-element.30), channel_id=1, source_target_pairs={{0,1},{1,2},{2,3},{3,4},{4,5},{5,6},{6,7},{7,8},{8,9},{9,10},{10,1... | collective-permute-start | bytes 1769480 | tf_op jit(solution)/shard_map/ppermute | solution.py:438
  71.1 9.2 %collective-permute-start.5 = (f32[512,128]{1,0:T(8,128)S(1)}, f32[512,128]{1,0:T(8,128)S(1)}, u32[]{:S(2)}, u32[]{:S(2)}) collective-permute-start(f32[512,128]{1,0:T(8,128)S(1)} %get-tuple-element.26), channel_id=1, source_target_pairs={{0,16},{16,32},{32,48},{48,64},{64,80},{80,96},{96,112},{1,17},{17... | collective-permute-start | bytes 786440 | tf_op jit(solution)/shard_map/ppermute | solution.py:438
  73.1 18.6 %collective-permute-start.4 = (f32[1024,128]{1,0:T(8,128)S(1)}, f32[1024,128]{1,0:T(8,128)S(1)}, u32[]{:S(2)}, u32[]{:S(2)}) collective-permute-start(f32[1024,128]{1,0:T(8,128)S(1)} %get-tuple-element.25), channel_id=1, source_target_pairs={{0,16},{16,32},{32,48},{48,64},{64,80},{80,96},{96,112},{1,17},{17... | collective-permute-start | bytes 1572872 | tf_op jit(solution)/shard_map/ppermute | solution.py:438
  78.4 13.3 %collective-permute-start.6 = (f32[1024,128]{1,0:T(8,128)S(1)}, f32[1024,128]{1,0:T(8,128)S(1)}, u32[]{:S(2)}, u32[]{:S(2)}) collective-permute-start(f32[1024,128]{1,0:T(8,128)S(1)} %get-tuple-element.27), channel_id=1, source_target_pairs={{16,0},{32,16},{48,32},{64,48},{80,64},{96,80},{112,96},{17,1},{33... | collective-permute-start | bytes 1572872 | tf_op jit(solution)/shard_map/ppermute | solution.py:438
  80.3 11.4 %collective-permute-start.7 = (f32[512,128]{1,0:T(8,128)S(1)}, f32[512,128]{1,0:T(8,128)S(1)}, u32[]{:S(2)}, u32[]{:S(2)}) collective-permute-start(f32[512,128]{1,0:T(8,128)S(1)} %get-tuple-element.28), channel_id=1, source_target_pairs={{16,0},{32,16},{48,32},{64,48},{80,64},{96,80},{112,96},{17,1},{33... | collective-permute-start | bytes 786440 | tf_op jit(solution)/shard_map/ppermute | solution.py:438

commit v3 on v2

--- a/solution.py
+++ b/solution.py
@@ -11,7 +11,7 @@
 axes = 3
 meta_rows = 8
 kinds = 4
-kept = 16
+kept = 28
 bf16 = jnp.bfloat16
 f32 = jnp.float32
 i32 = jnp.int32
@@ -226,12 +226,10 @@
             spread(k, at + 2, mixed0, partner0)
             return carry
 
-        @pl.when(turns > 0)
-        def _(k=k, turns=turns, turn=turn):
-            spread(k, 0, mixed0, partner0)
-            lax.fori_loop(0, turns >> 1, lambda t, c: turn(2 * t + 1, turn(2 * t, c)), 0)
-            lax.fori_loop(turns & ~1, turns, turn, 0)
-            finish(k, 2 * turns - 1, own1, far1)
+        spread(k, 0, mixed0, partner0)
+        lax.fori_loop(0, turns >> 1, lambda t, c, turn=turn: turn(2 * t + 1, turn(2 * t, c)), 0)
+        lax.fori_loop(turns & ~1, turns, turn, 0)
+        finish(k, 2 * turns - 1, own1, far1)
 
 
 def sorted_pairs(entries):

time: 93.3 us -> 92.2 us (0.988)
  the two profiles are of different devices: /device:TPU:7 before, /device:TPU:35 now
where the time goes in v3:
time: 92.2 us; the launch traced here: 90.7 us
  starting transfers between devices  44.3 us (48%)
  Pallas kernels  27.5 us (30%)
  waiting for transfers between devices  16.7 us (18%)
  other arithmetic  1.4 us (2%)
    ppermute x10, starting transfers between devices, shifted(): return lax.ppermute(x, axis, pairs)  44.3 us
    ppermute x10, waiting for transfers between devices, shifted(): return lax.ppermute(x, axis, pairs)  16.7 us
    pallas_call x1, Pallas kernels, column_call(): pl.pallas_call(lambda *refs: column_kernel(rows, total, last_row, *refs),...  9.08 us
    pallas_call x1, Pallas kernels, side_call(): pl.pallas_call(run, out_shape=(sds((axes - 1) * rows), sds(rows), sds(axe...  7.3 us
    pallas_call x1, Pallas kernels, level_call(): pl.pallas_call(lambda *refs: level_kernel(rows, total, last_row, *refs),...  6.8 us
  transfers between devices with their start and end apart: 10, of which 5 were waited for; matrix products, arithmetic and copies ran while one was open for 0% of the time, Pallas kernels for 19%

profile of v3, /device:TPU:35, one launch (start us, length us, event | category | flops | bytes accessed | tf_op | source)
XLA Modules:
  0.0 90.7 jit_solution(16224531196010308406)
XLA Ops:
  0.7 1.4 %note.1 = f32[8,128]{1,0:T(8,128)} custom-call(s32[1,1]{1,0:T(1,128)S(6)} %copy.11.count_ref, s32[1,256]{1,0:T(1,128)} %bitcast.11, s32[1,192]{1,0:T(1,128)} %bitcast.12, s32[1,192]{1,0:T(1,128)} %bitcast.13, s32[1,192]{1,0:T(1,128)} %bitcast.14), custom_call_target="tpu_custom_call" | custom-call | tf_op jit(solution)/shard_map/note/pallas_call | solution.py:526
  2.0 1.4 %pad_maximum_fusion.refs_0_.refs_1_ = f32[2568,128]{1,0:T(8,128)S(1)} fusion(f32[8,128]{1,0:T(8,128)} %note.1, f32[512,128]{1,0:T(8,128)} %bitcast.9, f32[512,128]{1,0:T(8,128)} %bitcast.10, f32[1536,128]{1,0:T(8,128)} %bitcast.8), kind=kLoop, calls=%fused_computation | loop fusion | flops 986112 | bytes 2629632 | tf_op jit(solution)/shard_map/concatenate | solution.py:536
  3.4 2.6 %collective-permute-start.1 = (f32[2568,128]{1,0:T(8,128)S(1)}, f32[2568,128]{1,0:T(8,128)S(1)}, u32[]{:S(2)}, u32[]{:S(2)}) collective-permute-start(f32[2568,128]{1,0:T(8,128)S(1)} %pad_maximum_fusion.refs_0_.refs_1_), channel_id=1, source_target_pairs={{16,0},{32,16},{48,32},{64,48},{80,64},{96,80},{112,96},{17,1},{33... | collective-permute-start | bytes 3944456 | tf_op jit(solution)/shard_map/ppermute | solution.py:436
  6.0 3.1 %collective-permute-start = (f32[2568,128]{1,0:T(8,128)S(1)}, f32[2568,128]{1,0:T(8,128)S(1)}, u32[]{:S(2)}, u32[]{:S(2)}) collective-permute-start(f32[2568,128]{1,0:T(8,128)S(1)} %pad_maximum_fusion.refs_0_.refs_1_), channel_id=1, source_target_pairs={{0,16},{16,32},{32,48},{48,64},{64,80},{80,96},{96,112},{1,17},{17... | collective-permute-start | bytes 3944456 | tf_op jit(solution)/shard_map/ppermute | solution.py:436
  9.1 1.3 %pack.1 = (f32[1928,128]{1,0:T(8,128)S(1)}, f32[1928,128]{1,0:T(8,128)S(1)}, f32[8,256]{1,0:T(8,128)S(1)}) custom-call(f32[2568,128]{1,0:T(8,128)S(1)} %pad_maximum_fusion.refs_0_.refs_1_), custom_call_target="tpu_custom_call" | custom-call | tf_op jit(solution)/shard_map/pack/pallas_call | solution.py:540
  10.4 3.5 %collective-permute-start.2 = (f32[1928,128]{1,0:T(8,128)S(1)}, f32[1928,128]{1,0:T(8,128)S(1)}, u32[]{:S(2)}, u32[]{:S(2)}) collective-permute-start(f32[1928,128]{1,0:T(8,128)S(1)} %get-tuple-element.19), channel_id=1, source_target_pairs={{0,1},{1,2},{2,3},{3,4},{4,5},{5,6},{6,7},{7,8},{8,9},{9,10},{10,1... | collective-permute-start | bytes 2961416 | tf_op jit(solution)/shard_map/ppermute | solution.py:436
  14.0 1.9 %collective-permute-start.3 = (f32[1928,128]{1,0:T(8,128)S(1)}, f32[1928,128]{1,0:T(8,128)S(1)}, u32[]{:S(2)}, u32[]{:S(2)}) collective-permute-start(f32[1928,128]{1,0:T(8,128)S(1)} %get-tuple-element.20), channel_id=1, source_target_pairs={{1,0},{2,1},{3,2},{4,3},{5,4},{6,5},{7,6},{8,7},{9,8},{10,9},{11,1... | collective-permute-start | bytes 2961416 | tf_op jit(solution)/shard_map/ppermute | solution.py:436
  15.9 6.8 %pairs_inside.1.refs_3_ = f32[1536,128]{1,0:T(8,128)S(1)} custom-call(f32[2568,128]{1,0:T(8,128)S(1)} %pad_maximum_fusion.refs_0_.refs_1_), custom_call_target="tpu_custom_call" | custom-call | tf_op jit(solution)/shard_map/pairs_inside/pallas_call | solution.py:472
  22.7 0.1 collective-permute-done.1.refs_2_
  22.8 0.9 collective-permute-done.refs_1_.refs_0_
  23.7 9.1 %pairs_column.1 = (f32[1536,128]{1,0:T(8,128)S(1)}, f32[1536,128]{1,0:T(8,128)S(1)}, f32[1536,128]{1,0:T(8,128)S(1)}) custom-call(f32[2568,128]{1,0:T(8,128)S(1)} %pad_maximum_fusion.refs_0_.refs_1_, f32[2568,128]{1,0:T(8,128)S(1)} %collective-permute-done.refs_1_.refs_0_, f32[2568,128]{1,0:T(8,128)S(1)} %collective-permute-done.1.refs_2_, ...), custom_call_target="tpu_custom_call" | custom-call | tf_op jit(solution)/shard_map/pairs_column/pallas_call | solution.py:485
  32.8 3.2 %collective-permute-done.2.refs_3_ = f32[1928,128]{1,0:T(8,128)S(1)} collective-permute-done((f32[1928,128]{1,0:T(8,128)S(1)}, f32[1928,128]{1,0:T(8,128)S(1)}, u32[]{:S(2)}, u32[]{:S(2)}) %collective-permute-start.2) | collective-permute-done | bytes 987168 | tf_op jit(solution)/shard_map/ppermute | solution.py:436
  36.0 3.6 %collective-permute-done.3.refs_4_ = f32[1928,128]{1,0:T(8,128)S(1)} collective-permute-done((f32[1928,128]{1,0:T(8,128)S(1)}, f32[1928,128]{1,0:T(8,128)S(1)}, u32[]{:S(2)}, u32[]{:S(2)}) %collective-permute-start.3) | collective-permute-done | bytes 987168 | tf_op jit(solution)/shard_map/ppermute | solution.py:436
  39.6 7.3 %pairs_side.1 = (f32[1024,128]{1,0:T(8,128)S(1)}, f32[512,128]{1,0:T(8,128)S(1)}, f32[1536,128]{1,0:T(8,128)S(1)}, f32[1024,128]{1,0:T(8,128)S(1)}, f32[512,128]...) custom-call(f32[2568,128]{1,0:T(8,128)S(1)} %collective-permute-done.refs_1_.refs_0_, ...), custom_call_target="tpu_custom_call" | custom-call | tf_op jit(solution)/shard_map/pairs_side/pallas_call | solution.py:502
  46.9 23.0 %collective-permute-start.8 = (f32[1152,128]{1,0:T(8,128)S(1)}, f32[1152,128]{1,0:T(8,128)S(1)}, u32[]{:S(2)}, u32[]{:S(2)}) collective-permute-start(f32[1152,128]{1,0:T(8,128)S(1)} %get-tuple-element.29), channel_id=1, source_target_pairs={{1,0},{2,1},{3,2},{4,3},{5,4},{6,5},{7,6},{8,7},{9,8},{10,9},{11,1... | collective-permute-start | bytes 1769480 | tf_op jit(solution)/shard_map/ppermute | solution.py:436
  69.9 1.9 %collective-permute-start.9 = (f32[1152,128]{1,0:T(8,128)S(1)}, f32[1152,128]{1,0:T(8,128)S(1)}, u32[]{:S(2)}, u32[]{:S(2)}) collective-permute-start(f32[1152,128]{1,0:T(8,128)S(1)} %get-tuple-element.30), channel_id=1, source_target_pairs={{0,1},{1,2},{2,3},{3,4},{4,5},{5,6},{6,7},{7,8},{8,9},{9,10},{10,1... | collective-permute-start | bytes 1769480 | tf_op jit(solution)/shard_map/ppermute | solution.py:436
  71.8 1.9 %collective-permute-start.5 = (f32[512,128]{1,0:T(8,128)S(1)}, f32[512,128]{1,0:T(8,128)S(1)}, u32[]{:S(2)}, u32[]{:S(2)}) collective-permute-start(f32[512,128]{1,0:T(8,128)S(1)} %get-tuple-element.26), channel_id=1, source_target_pairs={{0,16},{16,32},{32,48},{48,64},{64,80},{80,96},{96,112},{1,17},{17... | collective-permute-start | bytes 786440 | tf_op jit(solution)/shard_map/ppermute | solution.py:436
  73.8 1.9 %collective-permute-start.4 = (f32[1024,128]{1,0:T(8,128)S(1)}, f32[1024,128]{1,0:T(8,128)S(1)}, u32[]{:S(2)}, u32[]{:S(2)}) collective-permute-start(f32[1024,128]{1,0:T(8,128)S(1)} %get-tuple-element.25), channel_id=1, source_target_pairs={{0,16},{16,32},{32,48},{48,64},{64,80},{80,96},{96,112},{1,17},{17... | collective-permute-start | bytes 1572872 | tf_op jit(solution)/shard_map/ppermute | solution.py:436
  75.7 2.4 %collective-permute-start.6 = (f32[1024,128]{1,0:T(8,128)S(1)}, f32[1024,128]{1,0:T(8,128)S(1)}, u32[]{:S(2)}, u32[]{:S(2)}) collective-permute-start(f32[1024,128]{1,0:T(8,128)S(1)} %get-tuple-element.27), channel_id=1, source_target_pairs={{16,0},{32,16},{48,32},{64,48},{80,64},{96,80},{112,96},{17,1},{33... | collective-permute-start | bytes 1572872 | tf_op jit(solution)/shard_map/ppermute | solution.py:436
  78.1 0.0 collective-permute-done.5.refs_3_
  78.1 1.9 %collective-permute-start.7 = (f32[512,128]{1,0:T(8,128)S(1)}, f32[512,128]{1,0:T(8,128)S(1)}, u32[]{:S(2)}, u32[]{:S(2)}) collective-permute-start(f32[512,128]{1,0:T(8,128)S(1)} %get-tuple-element.28), channel_id=1, source_target_pairs={{16,0},{32,16},{48,32},{64,48},{80,64},{96,80},{112,96},{17,1},{33... | collective-permute-start | bytes 786440 | tf_op jit(solution)/shard_map/ppermute | solution.py:436
  80.1 8.9 %collective-permute-done.7.refs_5_ = f32[512,128]{1,0:T(8,128)S(1)} collective-permute-done((f32[512,128]{1,0:T(8,128)S(1)}, f32[512,128]{1,0:T(8,128)S(1)}, u32[]{:S(2)}, u32[]{:S(2)}) %collective-permute-start.7) | collective-permute-done | bytes 262176 | tf_op jit(solution)/shard_map/ppermute | solution.py:436
  89.0 0.0 collective-permute-done.4.refs_2_
  89.0 0.0 collective-permute-done.6.refs_4_
  89.0 0.0 collective-permute-done.8.refs_6_
  89.0 0.0 collective-permute-done.9.refs_7_
  89.0 1.7 %merge.1 = f32[1536,128]{1,0:T(8,128)} custom-call(f32[8,256]{1,0:T(8,128)S(1)} %get-tuple-element.18.refs_0_, f32[1536,128]{1,0:T(8,128)S(1)} %get-tuple-element.24.refs_1_, f32[1024,128]{1,0:T(8,128)S(1)} %collective-permute-done.4.refs_2_, f32[512,128]{1,0:T(8,128)S(1)} %collective-permute-done.5.refs_3_, f32[1024,128]{1,0:T(8,128)S(1)} %collective-permute-done.6.refs_4_, ...), custom_call_target="tpu_custom_call" | custom-call | tf_op jit(solution)/shard_map/merge/pallas_call | solution.py:558
Async XLA Ops:
  3.4 19.4 %collective-permute-start.1 = (f32[2568,128]{1,0:T(8,128)S(1)}, f32[2568,128]{1,0:T(8,128)S(1)}, u32[]{:S(2)}, u32[]{:S(2)}) collective-permute-start(f32[2568,128]{1,0:T(8,128)S(1)} %pad_maximum_fusion.refs_0_.refs_1_), channel_id=1, source_target_pairs={{16,0},{32,16},{48,32},{64,48},{80,64},{96,80},{112,96},{17,1},{33... | collective-permute-start | bytes 3944456 | tf_op jit(solution)/shard_map/ppermute | solution.py:436
  6.0 17.7 %collective-permute-start = (f32[2568,128]{1,0:T(8,128)S(1)}, f32[2568,128]{1,0:T(8,128)S(1)}, u32[]{:S(2)}, u32[]{:S(2)}) collective-permute-start(f32[2568,128]{1,0:T(8,128)S(1)} %pad_maximum_fusion.refs_0_.refs_1_), channel_id=1, source_target_pairs={{0,16},{16,32},{32,48},{48,64},{64,80},{80,96},{96,112},{1,17},{17... | collective-permute-start | bytes 3944456 | tf_op jit(solution)/shard_map/ppermute | solution.py:436
  10.4 25.6 %collective-permute-start.2 = (f32[1928,128]{1,0:T(8,128)S(1)}, f32[1928,128]{1,0:T(8,128)S(1)}, u32[]{:S(2)}, u32[]{:S(2)}) collective-permute-start(f32[1928,128]{1,0:T(8,128)S(1)} %get-tuple-element.19), channel_id=1, source_target_pairs={{0,1},{1,2},{2,3},{3,4},{4,5},{5,6},{6,7},{7,8},{8,9},{9,10},{10,1... | collective-permute-start | bytes 2961416 | tf_op jit(solution)/shard_map/ppermute | solution.py:436
  14.0 25.6 %collective-permute-start.3 = (f32[1928,128]{1,0:T(8,128)S(1)}, f32[1928,128]{1,0:T(8,128)S(1)}, u32[]{:S(2)}, u32[]{:S(2)}) collective-permute-start(f32[1928,128]{1,0:T(8,128)S(1)} %get-tuple-element.20), channel_id=1, source_target_pairs={{1,0},{2,1},{3,2},{4,3},{5,4},{6,5},{7,6},{8,7},{9,8},{10,9},{11,1... | collective-permute-start | bytes 2961416 | tf_op jit(solution)/shard_map/ppermute | solution.py:436
  46.9 42.1 %collective-permute-start.8 = (f32[1152,128]{1,0:T(8,128)S(1)}, f32[1152,128]{1,0:T(8,128)S(1)}, u32[]{:S(2)}, u32[]{:S(2)}) collective-permute-start(f32[1152,128]{1,0:T(8,128)S(1)} %get-tuple-element.29), channel_id=1, source_target_pairs={{1,0},{2,1},{3,2},{4,3},{5,4},{6,5},{7,6},{8,7},{9,8},{10,9},{11,1... | collective-permute-start | bytes 1769480 | tf_op jit(solution)/shard_map/ppermute | solution.py:436
  69.9 19.1 %collective-permute-start.9 = (f32[1152,128]{1,0:T(8,128)S(1)}, f32[1152,128]{1,0:T(8,128)S(1)}, u32[]{:S(2)}, u32[]{:S(2)}) collective-permute-start(f32[1152,128]{1,0:T(8,128)S(1)} %get-tuple-element.30), channel_id=1, source_target_pairs={{0,1},{1,2},{2,3},{3,4},{4,5},{5,6},{6,7},{7,8},{8,9},{9,10},{10,1... | collective-permute-start | bytes 1769480 | tf_op jit(solution)/shard_map/ppermute | solution.py:436
  71.8 6.3 %collective-permute-start.5 = (f32[512,128]{1,0:T(8,128)S(1)}, f32[512,128]{1,0:T(8,128)S(1)}, u32[]{:S(2)}, u32[]{:S(2)}) collective-permute-start(f32[512,128]{1,0:T(8,128)S(1)} %get-tuple-element.26), channel_id=1, source_target_pairs={{0,16},{16,32},{32,48},{48,64},{64,80},{80,96},{96,112},{1,17},{17... | collective-permute-start | bytes 786440 | tf_op jit(solution)/shard_map/ppermute | solution.py:436
  73.8 15.2 %collective-permute-start.4 = (f32[1024,128]{1,0:T(8,128)S(1)}, f32[1024,128]{1,0:T(8,128)S(1)}, u32[]{:S(2)}, u32[]{:S(2)}) collective-permute-start(f32[1024,128]{1,0:T(8,128)S(1)} %get-tuple-element.25), channel_id=1, source_target_pairs={{0,16},{16,32},{32,48},{48,64},{64,80},{80,96},{96,112},{1,17},{17... | collective-permute-start | bytes 1572872 | tf_op jit(solution)/shard_map/ppermute | solution.py:436
  75.7 13.3 %collective-permute-start.6 = (f32[1024,128]{1,0:T(8,128)S(1)}, f32[1024,128]{1,0:T(8,128)S(1)}, u32[]{:S(2)}, u32[]{:S(2)}) collective-permute-start(f32[1024,128]{1,0:T(8,128)S(1)} %get-tuple-element.27), channel_id=1, source_target_pairs={{16,0},{32,16},{48,32},{64,48},{80,64},{96,80},{112,96},{17,1},{33... | collective-permute-start | bytes 1572872 | tf_op jit(solution)/shard_map/ppermute | solution.py:436
  78.1 10.9 %collective-permute-start.7 = (f32[512,128]{1,0:T(8,128)S(1)}, f32[512,128]{1,0:T(8,128)S(1)}, u32[]{:S(2)}, u32[]{:S(2)}) collective-permute-start(f32[512,128]{1,0:T(8,128)S(1)} %get-tuple-element.28), channel_id=1, source_target_pairs={{16,0},{32,16},{48,32},{64,48},{80,64},{96,80},{112,96},{17,1},{33... | collective-permute-start | bytes 786440 | tf_op jit(solution)/shard_map/ppermute | solution.py:436
